TPU v7x, 128 devices: a whole 4x4x4 slice. The times are simulated.
128 devices in a mesh: grp: 8 (over y, core), tp: 16 (over x, z).
Axes of the slice: x: 4, y: 4, z: 4, core: 2. Of those that a mesh axis runs over, the one named last changes fastest.
Arguments:
- embedded: bfloat16 [2, 4096, 8192], P(None, 'grp', 'tp'), may hold values from -6 to 6
- norm_gain: float32 [8192], replicated, may hold values from 0.25 to 1.75
- w_query: bfloat16 [8192, 8192], P(None, 'tp'), may hold values from -0.0625 to 0.0625
- w_keyval: bfloat16 [8192, 2048], P(None, 'tp'), may hold values from -0.0625 to 0.0625
- w_out: bfloat16 [8192, 8192], P('tp'), may hold values from -0.75 to 0.75
- prefix_kv: bfloat16 [64, 512, 2048], P('grp', None, 'tp'), may hold values from -3000 to 3000
- prefix_len: int32 [64], replicated, may hold values from 64 to 512, as said below
- needed: int32 [8, 16], replicated, may hold values from 0 to 63, as said below
- row_slot: int32 [8, 512], P('grp'), may hold values from 0 to 15, never falling along the last dimension, each value on 1 to 64 neighbouring positions
Outputs:
- mixed: bfloat16 [2, 4096, 8192], P(None, 'grp', 'tp')
Inputs may be any that keep to these rules, and one draw needn't show every extreme that they name: `needed`: prefix p belongs to group p // 8. Each group lists 16 different prefixes; from one owner group it lists at most 2 prefixes p with p % 8 < 4 and at most 2 others, and in every group some owner group gives exactly 2 of each. `prefix_len`: prefix p has more than 256 tokens exactly when p % 8 < 4. Some prefix has exactly 512 tokens. `row_slot`: within each group the rows are sorted by slot; every slot has 1 to 64 rows, exactly 64 in some slot.
All inputs are finite; a program needn't handle non-finite values.
Results may differ from a plain program's by a relative error of at most 0.02.
Values may be sent and summed in bfloat16 or wider, within the bound.
A program may use at most 128 MiB of HBM per device.

v0:
```python
import math

import jax
import jax.numpy as jnp
from jax import lax
from jax.sharding import PartitionSpec as P

HEAD = 128
CAP = 4
MOST = 64


EPSILON = 1e-05
ROPE_THETA = 500000.0


def swapped(block, axis, apart):
    count = lax.axis_size(axis)
    route = []
    for low in range(count):
        high = low | 1 << apart
        if high != low and high < count:
            route += [(low, high), (high, low)]
    return lax.ppermute(block, axis, route)


def rotate(values, positions, first_dim):
    half_count = values.shape[-1] // 2
    pair_index = (first_dim // 2 + jnp.arange(half_count)).astype(jnp.float32)
    inverse = jnp.exp(pair_index * (-2.0 * math.log(ROPE_THETA) / HEAD))
    angle = positions.astype(jnp.float32)[:, None, None] * inverse[None, None, :]
    cosine = jnp.cos(angle)
    sine = jnp.sin(angle)
    evens = values[..., 0::2]
    odds = values[..., 1::2]
    turned = jnp.stack([evens * cosine - odds * sine, evens * sine + odds * cosine], axis=-1)
    return turned.reshape(values.shape)


def join_parts(key_part, value_part, member_index, split_count):
    bit_level = 0
    while 1 << bit_level < split_count:
        other_keys, other_values = swapped((key_part, value_part), "tp", bit_level)
        is_upper = member_index >> bit_level & 1 == 1
        key_part = jnp.where(
            is_upper,
            jnp.concatenate([other_keys, key_part], axis=-1),
            jnp.concatenate([key_part, other_keys], axis=-1),
        )
        value_part = jnp.where(
            is_upper,
            jnp.concatenate([other_values, value_part], axis=-1),
            jnp.concatenate([value_part, other_values], axis=-1),
        )
        bit_level += 1
    return (key_part, value_part)


def pick_ranked(flags, values, slots):
    ranks = jnp.cumsum(flags, axis=1) - 1
    selected = (flags[:, :, None] == 1) & (ranks[:, :, None] == jnp.arange(slots)[None, None, :])
    return jnp.sum(jnp.where(selected, values[:, :, None], 0), axis=1)


def earlier_count(flags, owners):
    slot_ids = jnp.arange(owners.shape[0])
    earlier = (
        (slot_ids[None, :] < slot_ids[:, None])
        & (owners[None, :] == owners[:, None])
        & (flags[None, :] == 1)
    )
    return jnp.sum(earlier.astype(jnp.int32), axis=1)


def body(embedded, norm_gain, w_query, w_keyval, w_out, prefix_kv, prefix_len, needed, row_slot):
    group_count = lax.axis_size("grp")
    group_index = lax.axis_index("grp")
    member_index = lax.axis_index("tp")
    step_count, row_count, width_part = embedded.shape
    heads_here = w_query.shape[1] // HEAD
    part_width = w_keyval.shape[1] // 2
    split_count = HEAD // part_width
    owned_count, length_count, kv_width = prefix_kv.shape
    need_count = needed.shape[1]
    prefix_count = prefix_len.shape[0]
    inv_sqrt = 1.0 / math.sqrt(HEAD)
    slot_of_row = row_slot[0]
    my_list = lax.dynamic_index_in_dim(needed, group_index, 0, keepdims=False)
    owner_group = needed // owned_count
    local_id = needed - owner_group * owned_count
    is_mine = (owner_group == group_index).astype(jnp.int32)
    send_ids = pick_ranked(is_mine, local_id, CAP)
    outgoing = prefix_kv[send_ids.reshape(-1)].reshape(group_count, CAP, length_count, kv_width)
    incoming = lax.all_to_all(outgoing, "grp", split_axis=0, concat_axis=0, tiled=True).reshape(
        group_count * CAP, length_count, kv_width
    )
    my_owner = my_list // owned_count
    every_slot = jnp.ones((need_count,), jnp.int32)
    source_index = my_owner * CAP + earlier_count(every_slot, my_owner)
    chosen = incoming[source_index]
    key_cache, value_cache = join_parts(
        chosen[..., :part_width], chosen[..., part_width:], member_index, split_count
    )
    prefix_match = my_list[:, None] == jnp.arange(prefix_count)[None, :]
    slot_len = jnp.sum(jnp.where(prefix_match, prefix_len[None, :], 0), axis=1)
    row_match = slot_of_row[:, None] == jnp.arange(need_count)[None, :]
    row_len = jnp.sum(jnp.where(row_match, slot_len[None, :], 0), axis=1)
    before_slot = (slot_of_row[None, :] < jnp.arange(need_count)[:, None]).astype(jnp.int32)
    first_rows = jnp.minimum(jnp.sum(before_slot, axis=1), row_count - MOST)
    key_first = member_index % split_count * part_width
    own_keys = []
    own_values = []
    outputs = []
    for step_index in range(step_count):
        stream_rows = embedded[step_index]
        whole = lax.all_gather(stream_rows, "tp", axis=1, tiled=True).astype(jnp.float32)
        inv_rms = lax.rsqrt(jnp.mean(whole * whole, axis=1, keepdims=True) + EPSILON)
        normed = (whole * inv_rms * norm_gain[None, :]).astype(jnp.bfloat16)
        query_sum = jnp.dot(normed, w_query, preferred_element_type=jnp.float32)
        keyval_sum = jnp.dot(normed, w_keyval, preferred_element_type=jnp.float32)
        positions = row_len + step_index
        queries = rotate(query_sum.reshape(row_count, heads_here, HEAD), positions, 0).astype(
            jnp.bfloat16
        )
        new_key = rotate(
            keyval_sum[:, :part_width].reshape(row_count, 1, part_width), positions, key_first
        )
        new_key = new_key.reshape(row_count, part_width).astype(jnp.bfloat16)
        new_value = keyval_sum[:, part_width:].astype(jnp.bfloat16)
        new_key, new_value = join_parts(new_key, new_value, member_index, split_count)
        own_keys.append(new_key)
        own_values.append(new_value)
        key_stack = jnp.stack(own_keys)
        value_stack = jnp.stack(own_values)

        def attend_slot(slot_index, attended):
            first_row = first_rows[slot_index]
            query_block = lax.dynamic_slice_in_dim(queries, first_row, MOST, 0)
            keys_here = lax.dynamic_index_in_dim(key_cache, slot_index, 0, keepdims=False)
            values_here = lax.dynamic_index_in_dim(value_cache, slot_index, 0, keepdims=False)
            scores = (
                jnp.einsum(
                    "rhd,ld->rhl", query_block, keys_here, preferred_element_type=jnp.float32
                )
                * inv_sqrt
            )
            in_range = jnp.arange(length_count)[None, None, :] < slot_len[slot_index]
            scores = jnp.where(in_range, scores, -jnp.inf)
            own_key_block = lax.dynamic_slice_in_dim(key_stack, first_row, MOST, 1)
            own_value_block = lax.dynamic_slice_in_dim(value_stack, first_row, MOST, 1)
            own_scores = (
                jnp.einsum(
                    "rhd,srd->rhs", query_block, own_key_block, preferred_element_type=jnp.float32
                )
                * inv_sqrt
            )
            row_max = jnp.maximum(jnp.max(scores, axis=-1), jnp.max(own_scores, axis=-1))[..., None]
            weights = jnp.exp(scores - row_max)
            own_weights = jnp.exp(own_scores - row_max)
            denominator = jnp.sum(weights, axis=-1) + jnp.sum(own_weights, axis=-1)
            summed = jnp.einsum(
                "rhl,ld->rhd",
                weights.astype(jnp.bfloat16),
                values_here,
                preferred_element_type=jnp.float32,
            )
            summed = summed + jnp.einsum(
                "rhs,srd->rhd",
                own_weights.astype(jnp.bfloat16),
                own_value_block,
                preferred_element_type=jnp.float32,
            )
            block_out = (
                (summed / denominator[..., None])
                .astype(jnp.bfloat16)
                .reshape(MOST, heads_here * HEAD)
            )
            in_slot = lax.dynamic_slice_in_dim(slot_of_row, first_row, MOST, 0) == slot_index
            previous = lax.dynamic_slice_in_dim(attended, first_row, MOST, 0)
            return lax.dynamic_update_slice_in_dim(
                attended, jnp.where(in_slot[:, None], block_out, previous), first_row, 0
            )

        attended = lax.fori_loop(
            0, need_count, attend_slot, jnp.zeros((row_count, heads_here * HEAD), jnp.bfloat16)
        )
        partial_out = jnp.dot(attended, w_out, preferred_element_type=jnp.float32)
        shared = lax.psum_scatter(
            partial_out.astype(jnp.bfloat16), "tp", scatter_dimension=1, tiled=True
        ).astype(jnp.float32)
        outputs.append((stream_rows.astype(jnp.float32) + shared).astype(jnp.bfloat16))
    return jnp.stack(outputs)


def solution(mesh):
    in_specs = (
        P(None, "grp", "tp"),
        P(),
        P(None, "tp"),
        P(None, "tp"),
        P("tp", None),
        P("grp", None, "tp"),
        P(),
        P(),
        P("grp", None),
    )
    out_specs = P(None, "grp", "tp")
    return jax.shard_map(body, mesh=mesh, in_specs=in_specs, out_specs=out_specs, check_vma=False)
```

profile of v0, /device:TPU:0, one launch (start us, length us, event | category | flops | bytes accessed | tf_op | source)
XLA Modules:
  0.0 605.6 jit_solution(11439078832132483718)
XLA Ops:
  6.5 2.4 fusion.95
  11.6 4.3 gather_fusion
  15.9 4.6 all-to-all-start
  21.5 48.8 %all-to-all-done = bf16[8,4,512,128]{3,2,1,0:T(8,128)(2,1)} async-done(((bf16[8,4,512,128]{3,2,1,0:T(8,128)(2,1)}), bf16[8,4,512,128]{3,2,1,0:T(8,128)(2,1)}, u32[]{:S(2)}, u32[]{:S(2)}) %all-to-all-start) | async-done | bytes 4194336 | tf_op jit(solution)/shard_map/all_to_all | solution.py:94
  70.2 4.3 gather_fusion.1
  74.6 5.0 fusion.94
  79.6 2.7 copy.143
  82.4 2.0 collective-permute-start.2
  84.3 2.7 copy.138
  89.1 1.7 multiply_sine_fusion.1
  90.8 21.2 %collective-permute-done.2 = bf16[16,512,64]{1,2,0:T(8,128)(2,1)S(1)} collective-permute-done((bf16[16,512,64]{1,2,0:T(8,128)(2,1)}, bf16[16,512,64]{1,2,0:T(8,128)(2,1)S(1)}, u32[]{:S(2)}, u32[]{:S(2)}) %collective-permute-start.2) | collective-permute-done | bytes 1048608 | tf_op jit(solution)/shard_map/ppermute | solution.py:24
  111.9 1.8 copy.144
  113.7 29.3 %collective-permute-done = bf16[16,512,64]{1,2,0:T(8,128)(2,1)} collective-permute-done((bf16[16,512,64]{1,2,0:T(8,128)(2,1)}, bf16[16,512,64]{1,2,0:T(8,128)(2,1)}, u32[]{:S(2)}, u32[]{:S(2)}) %collective-permute-start) | collective-permute-done | bytes 1048608 | tf_op jit(solution)/shard_map/ppermute | solution.py:24
  143.0 2.9 copy.139
  145.9 7.2 %maximum_select_fusion.1 = bf16[16,512,128]{2,1,0:T(8,128)(2,1)} fusion(bf16[16,512,64]{2,1,0:T(8,128)(2,1)} %get-tuple-element.517, bf16[16,512,64]{2,1,0:T(8,128)(2,1)} %copy.144, pred[]{:T(512)S(6)} %eq.109), kind=kLoop, calls=%fused_computation.79 | loop fusion | flops 9437184 | bytes 4194305 | tf_op jit(solution)/shard_map/jit(_where)/select_n | solution.py:50
  153.1 7.3 %maximum_select_fusion = bf16[16,512,128]{2,1,0:T(8,128)(2,1)} fusion(bf16[16,512,64]{2,1,0:T(8,128)(2,1)} %get-tuple-element.518, bf16[16,512,64]{2,1,0:T(8,128)(2,1)} %copy.139, pred[]{:T(512)S(6)} %eq.109), kind=kLoop, calls=%fused_computation.78 | loop fusion | flops 9437184 | bytes 4194305 | tf_op jit(solution)/shard_map/jit(_where)/select_n | solution.py:45
  160.3 5.3 fusion.42
  166.1 3.1 fusion.52
  170.0 12.0 %all-gather.7.cloned.1.call-done = bf16[1,512,8192]{2,1,0:T(8,128)(2,1)} async-done(((bf16[1,512,512]{2,1,0:T(8,128)(2,1)}), bf16[1,512,8192]{2,1,0:T(8,128)(2,1)}) %all-gather.7.cloned.1.call-update) | async-done | bytes 8388624 | tf_op jit(solution)/shard_map/all_gather | solution.py:116
  182.0 5.3 fusion.45
  187.8 3.3 fusion.48
  195.2 11.4 %fusion.54 = f32[512,512]{0,1:T(8,128)S(1)} fusion(bf16[8192,512]{1,0:T(8,128)(2,1)} %param.15, bf16[1,512,8192]{2,1,0:T(8,128)(2,1)} %all-gather.5.cloned.1.call-done, f32[8192]{0:T(1024)S(1)} %copy-done.11, f32[512]{0:T(512)S(1)} %add_rsqrt_fusion.1), kind=kOutput, calls=%fused_computation.77 | convolution fusion | flops 4311744512 | bytes 17860608 | tf_op jit(solution)/shard_map/dot_general | solution.py:119
  207.1 11.4 %fusion.50 = f32[512,512]{0,1:T(8,128)S(1)} fusion(bf16[8192,512]{1,0:T(8,128)(2,1)} %param.15, bf16[1,512,8192]{2,1,0:T(8,128)(2,1)} %all-gather.7.cloned.1.call-done, f32[512]{0:T(512)S(1)} %add_rsqrt_fusion, f32[8192]{0:T(1024)} %param.14), kind=kOutput, calls=%fused_computation.75 | convolution fusion | flops 4311744512 | bytes 17860608 | tf_op jit(solution)/shard_map/dot_general | solution.py:119
  225.2 1.6 collective-permute-start.4
  227.4 2.4 fusion.60
  230.7 1.7 collective-permute-start.3
  238.1 130.9 %while.27 = (s32[]{:T(128)}, bf16[512,512]{1,0:T(8,128)(2,1)S(1)}, s32[16]{0:T(128)S(1)}, s32[512]{0:T(512)S(1)}, s32[16]{0:T(128)S(1)}, /*index=5*/bf16[512,4,1...) while((s32[]{:T(128)}, bf16[512,512]{1,0:T(8,128)(2,1)S(1)}, ...), condition=%wide.region_18.19_spmd, body=%wide.region_13.18_spmd.sunk | while | flops 68422720 | bytes 2943575 | solution.py:184
  369.1 10.1 %convolution_convert_fusion = bf16[512,8192]{1,0:T(8,128)(2,1)} fusion(bf16[512,512]{1,0:T(8,128)(2,1)S(1)} %get-tuple-element.344, bf16[512,8192]{1,0:T(8,128)(2,1)} %param.17), kind=kOutput, calls=%fused_computation.72 | convolution fusion | flops 4299161600 | bytes 17301504 | tf_op jit(solution)/shard_map/dot_general | solution.py:187
  379.3 122.1 %while.26 = (s32[]{:T(128)}, bf16[512,512]{1,0:T(8,128)(2,1)S(1)}, s32[16]{0:T(128)S(1)}, s32[512]{0:T(512)S(1)}, s32[16]{0:T(128)S(1)}, /*index=5*/bf16[512,4,1...) while((s32[]{:T(128)}, bf16[512,512]{1,0:T(8,128)(2,1)S(1)}, ...), condition=%wide.region_10.11_spmd, body=%wide.region_7.10_spmd.sunk | while | flops 68266048 | bytes 2641495 | solution.py:184
  501.4 10.2 %convolution_convert_fusion.1 = bf16[512,8192]{1,0:T(8,128)(2,1)} fusion(bf16[512,512]{1,0:T(8,128)(2,1)S(1)} %get-tuple-element.343, bf16[512,8192]{1,0:T(8,128)(2,1)} %param.17), kind=kOutput, calls=%fused_computation.73 | convolution fusion | flops 4299161600 | bytes 17301504 | tf_op jit(solution)/shard_map/dot_general | solution.py:187
  511.7 84.5 %reduce-scatter.3.cloned.1.call-done = bf16[512,512]{1,0:T(8,128)(2,1)} async-done(((bf16[512,8192]{1,0:T(8,128)(2,1)}), bf16[512,512]{1,0:T(8,128)(2,1)}) %reduce-scatter.3.cloned.1.call-update) | async-done | bytes 524304 | tf_op jit(solution)/shard_map/reduce_scatter | solution.py:188
  596.2 2.4 fusion.58
  (650 shorter events, 213.9 us)
Async XLA Ops:
  6.5 159.1 %copy-start = (bf16[8192,128]{1,0:T(8,128)(2,1)S(1)}, bf16[8192,128]{1,0:T(8,128)(2,1)}, u32[]{:S(2)}) copy-start(bf16[8192,128]{1,0:T(8,128)(2,1)} %param.16) | copy-start | bytes 6291460
  6.5 153.8 %all-gather.5.cloned.1.call-start = ((), (), s32[]{:S(2)}) async-start(), calls=%async_computation.5 | async-start | bytes 8912896 | tf_op jit(solution)/shard_map/all_gather | solution.py:116
  9.0 173.0 %all-gather.7.cloned.1.call-start = ((), (), s32[]{:S(2)}) async-start(), calls=%async_computation.6 | async-start | bytes 8912896 | tf_op jit(solution)/shard_map/all_gather | solution.py:116
  15.9 54.3 %all-to-all-start = ((bf16[8,4,512,128]{3,2,1,0:T(8,128)(2,1)}), bf16[8,4,512,128]{3,2,1,0:T(8,128)(2,1)}, u32[]{:S(2)}, u32[]{:S(2)}) async-start(bf16[8,4,512,128]{3,2,1,0:T(8,128)(2,1)} %bitcast.189), calls=%async_computation | async-start | bytes 8388608 | tf_op jit(solution)/shard_map/all_to_all | solution.py:94
  20.5 491.2 %reduce-scatter.5.cloned.1.call-start = ((), (), s32[]{:S(2)}) async-start(), calls=%async_computation.4 | async-start | bytes 8912896 | tf_op jit(solution)/shard_map/reduce_scatter | solution.py:188
  74.6 13.0 %copy-start.7 = (s32[1,512]{1,0:T(1,128)S(1)}, s32[1,512]{1,0:T(1,128)}, u32[]{:S(2)}) copy-start(s32[1,512]{1,0:T(1,128)} %param.21) | copy-start | bytes 6148
  74.6 13.1 %copy-start.12 = (s32[64]{0:T(128)S(1)}, s32[64]{0:T(128)}, u32[]{:S(2)}) copy-start(s32[64]{0:T(128)} %param.19) | copy-start | bytes 772
  82.4 29.6 %collective-permute-start.2 = (bf16[16,512,64]{1,2,0:T(8,128)(2,1)}, bf16[16,512,64]{1,2,0:T(8,128)(2,1)S(1)}, u32[]{:S(2)}, u32[]{:S(2)}) collective-permute-start(bf16[16,512,64]{1,2,0:T(8,128)(2,1)} %copy.143), channel_id=1, source_target_pairs={{0,1},{1,0},{2,3},{3,2},{4,5},{5,4},{6,7},{7,6},{8,9},{9,8},{10,11... | collective-permute-start | bytes 3145736 | tf_op jit(solution)/shard_map/ppermute | solution.py:24
  87.0 56.0 %collective-permute-start = (bf16[16,512,64]{1,2,0:T(8,128)(2,1)}, bf16[16,512,64]{1,2,0:T(8,128)(2,1)}, u32[]{:S(2)}, u32[]{:S(2)}) collective-permute-start(bf16[16,512,64]{1,2,0:T(8,128)(2,1)} %copy.138), channel_id=1, source_target_pairs={{0,1},{1,0},{2,3},{3,2},{4,5},{5,4},{6,7},{7,6},{8,9},{9,8},{10,11... | collective-permute-start | bytes 3145736 | tf_op jit(solution)/shard_map/ppermute | solution.py:24
  87.9 0.6 copy-start.9
  153.1 12.5 %copy-start.11 = (f32[8192]{0:T(1024)S(1)}, f32[8192]{0:T(1024)}, u32[]{:S(2)}) copy-start(f32[8192]{0:T(1024)} %param.14) | copy-start | bytes 98308
  160.3 5.8 copy-start.2
  169.2 0.7 copy-start.5
  182.0 5.8 copy-start.3
  187.8 4.1 copy-start.8
  191.1 0.7 copy-start.6
  218.5 19.6 %copy-start.10 = (s32[16]{0:T(128)S(1)}, s32[16]{0:T(128)}, u32[]{:S(2)}) copy-start(s32[16]{0:T(128)} %copy-done.9) | copy-start | bytes 196
  218.5 19.6 %copy-start.13 = (s32[16]{0:T(128)S(1)}, s32[16]{0:T(128)}, u32[]{:S(2)}) copy-start(s32[16]{0:T(128)} %broadcast_minimum_fusion) | copy-start | bytes 196
  225.2 9.5 %collective-permute-start.4 = (bf16[512,64]{0,1:T(8,128)(2,1)}, bf16[512,64]{0,1:T(8,128)(2,1)}, u32[]{:S(2)}, u32[]{:S(2)}) collective-permute-start(bf16[512,64]{0,1:T(8,128)(2,1)} %convert_element_type.177), channel_id=1, source_target_pairs={{0,1},{1,0},{2,3},{3,2},{4,5},{5,4},{6,7},{7,6},{8,9},{9,8},{10,11... | collective-permute-start | bytes 196616 | tf_op jit(solution)/shard_map/ppermute | solution.py:24
  226.8 6.7 %collective-permute-start.1 = (bf16[512,64]{0,1:T(8,128)(2,1)}, bf16[512,64]{0,1:T(8,128)(2,1)}, u32[]{:S(2)}, u32[]{:S(2)}) collective-permute-start(bf16[512,64]{0,1:T(8,128)(2,1)} %convert_element_type.168), channel_id=1, source_target_pairs={{0,1},{1,0},{2,3},{3,2},{4,5},{5,4},{6,7},{7,6},{8,9},{9,8},{10,11... | collective-permute-start | bytes 196616 | tf_op jit(solution)/shard_map/ppermute | solution.py:24
  230.7 5.2 collective-permute-start.3
  232.4 4.5 collective-permute-start.5
  379.2 217.0 %reduce-scatter.3.cloned.1.call-start = ((), (), s32[]{:S(2)}) async-start(), calls=%async_computation.3 | async-start | bytes 8912896 | tf_op jit(solution)/shard_map/reduce_scatter | solution.py:188
  501.4 97.2 %copy-start.1 = (bf16[8192,128]{1,0:T(8,128)(2,1)S(1)}, bf16[8192,128]{1,0:T(8,128)(2,1)}, u32[]{:S(2)}) copy-start(bf16[8192,128]{1,0:T(8,128)(2,1)} %param.16) | copy-start | bytes 6291460
  511.6 84.6 %copy-start.4 = (bf16[2,512,512]{2,1,0:T(8,128)(2,1)S(1)}, bf16[2,512,512]{2,1,0:T(8,128)(2,1)}, u32[]{:S(2)}) copy-start(bf16[2,512,512]{2,1,0:T(8,128)(2,1)} %param.13) | copy-start | bytes 3145732
Sparse Core Ops, SparseCore 0:
  9.5 83.6 all-gather.4
  95.3 86.6 all-gather.6
  379.3 84.6 reduce-scatter.4
  511.7 84.3 reduce-scatter.2
where the time goes:
time: 613 us; the launch traced here: 606 us
  waiting for transfers between devices  196 us (32%)
  matrix products  138 us (23%)
  local copies, waits for them, and re-layouts  104 us (17%)
  other arithmetic  76.7 us (13%)
  loops' own time  65 us (11%)
  between operations  14 us (2%)
  starting transfers between devices  11.1 us (2%)
    reduce_scatter x2, waiting for transfers between devices, body(): lax.psum_scatter(partial_out.astype(jnp.bfloat16), 'tp', scatter_dimensio...  84.5 us
    another operation x2, loops' own time, body(): lax.fori_loop(0, need_count, attend_slot, jnp.zeros((row_count, heads_her...  65 us
    ppermute x6, waiting for transfers between devices, swapped(): return lax.ppermute(block, axis, route)  50.4 us
    all_to_all x1, waiting for transfers between devices, body(): lax.all_to_all(outgoing, 'grp', split_axis=0, concat_axis=0, tiled=True)  48.8 us
    dot_general x32, matrix products, attend_slot(): jnp.einsum('rhd,ld->rhl', query_block, keys_here, preferred_element_type=...  39 us
    dot_general x32, matrix products, attend_slot(): jnp.einsum('rhl,ld->rhd', weights.astype(jnp.bfloat16), values_here, pref...  38.5 us
    dot_general x2, matrix products, body(): query_sum = jnp.dot(normed, w_query, preferred_element_type=jnp.float32)  22.7 us
    lt x32, other arithmetic, attend_slot(): in_range = jnp.arange(length_count)[None, None, :] < slot_len[slot_index]  20.8 us
  transfers between devices with their start and end apart: 11, of which 5 were waited for; matrix products, arithmetic and copies ran while one was open for 26% of the time, Pallas kernels for 0%

commit v1 on v0

v1 whole, which is shorter than its diff:
```python
import functools
import math

import jax
import jax.numpy as jnp
from jax import lax
from jax.experimental import pallas as pl
from jax.experimental.pallas import tpu as pltpu
from jax.sharding import PartitionSpec as P

HEAD = 128
HALF = 64
RING = 4
EPSILON = 1e-05
ROPE_THETA = 500000.0
SUB = 32
MIB = 1 << 20
MESH = pl.DeviceIdType.MESH
ORDER = (0, 3, 1, 2)


def place():
    t = lax.axis_index("tp")
    return t, lax.div(t, RING), lax.rem(t, RING)


def index_of(x, z):
    return lax.rem(x, RING) * RING + lax.rem(z, RING)


def greet(x, z):
    barrier = pltpu.get_barrier_semaphore()
    for a, b in ((1, 0), (3, 0), (0, 1), (0, 3)):
        pl.semaphore_signal(
            barrier, inc=1, device_id={"tp": index_of(x + a, z + b)}, device_id_type=MESH
        )
    pl.semaphore_wait(barrier, 4)


def project_kernel(
    emb, wq, wkv, gain, table, slots, q_out, kv_out,
    blocks, w, acc, squares, cosine, sine, kv_other,
    load_sem, w_sem, send_sem, recv_sem, kv_sem,
):
    rows, width = emb.shape[1], emb.shape[2]
    half = rows // 2
    q_cols = wq.shape[1]
    t, x, z = place()

    def slot_of(s, along, across):
        return index_of(x + across, z + along) if s == 0 else index_of(x + along, z + across)

    def neighbour(s, phase, d):
        on_z = (s == 0) == (phase == 0)
        return {"tp": index_of(x, z + d) if on_z else index_of(x + d, z)}

    def move(s, phase, o, kind, slot, d):
        ref = blocks.at[s, slot]
        if kind == 2:
            ref = blocks.at[s, slot, pl.ds(0, half)]
        if kind == 3:
            ref = blocks.at[s, slot, pl.ds(half, half)]
        i = o if phase else RING
        return pltpu.make_async_remote_copy(
            src_ref=ref,
            dst_ref=ref,
            send_sem=send_sem.at[s, i, kind],
            recv_sem=recv_sem.at[s, i, kind],
            device_id=neighbour(s, phase, d),
            device_id_type=MESH,
        )

    def at(s, phase, o, far):
        return slot_of(s, far, 0) if phase == 0 else slot_of(s, ORDER[o], far)

    started = []

    def start(*a):
        copy = move(*a)
        copy.start()
        started.append(copy)

    def send(s, phase, o):
        slot = at(s, phase, o, 0)
        start(s, phase, o, 0, slot, 1)
        start(s, phase, o, 1, slot, RING - 1)

    def pass_on(s, phase, o):
        back, ahead = at(s, phase, o, 3), at(s, phase, o, 1)
        move(s, phase, o, 0, back, 1).wait_recv()
        start(s, phase, o, 2, back, 1)
        move(s, phase, o, 1, ahead, 1).wait_recv()
        start(s, phase, o, 3, ahead, RING - 1)

    def opposite(s, phase, o):
        slot = at(s, phase, o, 2)
        move(s, phase, o, 2, slot, 1).wait_recv()
        move(s, phase, o, 3, slot, 1).wait_recv()

    def multiply(*todo):
        def one(i, _):
            which = lax.div(i, 2)
            s, slot = jnp.int32(todo[0][0]), todo[0][1]
            for j in range(1, len(todo)):
                s = jnp.where(which == j, todo[j][0], s)
                slot = jnp.where(which == j, todo[j][1], slot)
            r = pl.ds(pl.multiple_of(lax.rem(i, 2) * half, half), half)
            value = blocks[s, slot, r, :].astype(jnp.float32)
            square = value * value
            total = square[:, :128]
            for c in range(1, width // 128):
                total = total + square[:, c * 128 : (c + 1) * 128]
            squares[s, r, :] += total
            scaled = (value * gain[pl.ds(slot, 1), :]).astype(jnp.bfloat16)
            depth = pl.ds(pl.multiple_of(slot * width, width), width)
            acc[s, r, :] += jnp.dot(scaled, w[depth, :], preferred_element_type=jnp.float32)
            return 0

        lax.fori_loop(0, 2 * len(todo), one, 0)

    greet(x, z)
    loads = [pltpu.make_async_copy(emb.at[s], blocks.at[s, t], load_sem.at[s]) for s in (0, 1)]
    for copy in loads:
        copy.start()
    weights = [
        pltpu.make_async_copy(wq, w.at[:, pl.ds(0, q_cols)], w_sem.at[0]),
        pltpu.make_async_copy(wkv, w.at[:, pl.ds(q_cols, 2 * HALF)], w_sem.at[1]),
    ]
    for copy in loads:
        copy.wait()
    for s in (0, 1):
        send(s, 0, 0)
    for copy in weights:
        copy.start()
    for s in (0, 1):
        send(s, 1, 0)
    acc[...] = jnp.zeros_like(acc)
    squares[...] = jnp.zeros_like(squares)

    def spread(i, _):
        s, r = lax.div(i, 4), pl.ds(pl.multiple_of(lax.rem(i, 4) * 128, 128), 128)
        slot_here = jnp.broadcast_to(slots[r, :], (128, HEAD))
        for k, ref in ((0, cosine), (1, sine)):
            out = jnp.zeros((128, HEAD), jnp.float32)
            for n in range(table.shape[2]):
                out = jnp.where(slot_here == n, table[k, s, n : n + 1, :], out)
            ref[s, r, :] = out
        return 0

    lax.fori_loop(0, 8, spread, 0)
    for copy in weights:
        copy.wait()
    both = (0, 1)
    multiply((0, t), (1, t))
    for s in both:
        pass_on(s, 0, 0)
    for s in both:
        send(s, 1, 1)
    for s in both:
        send(s, 1, 2)
    multiply(*[(s, at(s, 0, 0, d)) for d in (3, 1) for s in both])
    for s in both:
        pass_on(s, 1, 0)
    multiply(*[(s, at(s, 1, 0, d)) for d in (3, 1) for s in both])
    for s in both:
        opposite(s, 0, 0)
        send(s, 1, 3)
    multiply(*[(s, at(s, 0, 0, 2)) for s in both])
    for o in (1, 2, 3):
        for s in both:
            pass_on(s, 1, o)
        multiply(*[(s, at(s, 1, o, d)) for d in (3, 1) for s in both])
        for s in both:
            opposite(s, 1, o - 1)
        multiply(*[(s, at(s, 1, o - 1, 2)) for s in both])
    for s in both:
        opposite(s, 1, 3)
    multiply(*[(s, at(s, 1, 3, 2)) for s in both])

    upper = lax.rem(t, 2)
    lane = lax.broadcasted_iota(jnp.int32, (128, HEAD), 1)
    low = lane < HALF
    even = lax.rem(lane, 2) == 0

    def turn(v, c, n):
        other = jnp.where(even, pltpu.roll(v, HEAD - 1, 1), pltpu.roll(v, 1, 1))
        return v * c + other * n

    def scale_of(s, r):
        mean = jnp.sum(squares[s, r, :], axis=1, keepdims=True) / (RING * RING * width)
        return lax.rsqrt(mean + EPSILON)

    def own_kv(i, _):
        s, r = lax.div(i, 4), pl.ds(pl.multiple_of(lax.rem(i, 4) * 128, 128), 128)
        v = acc[s, r, pl.ds(q_cols, HEAD)] * scale_of(s, r)
        c, n = cosine[s, r, :], sine[s, r, :]
        c = jnp.where(upper == 0, c, pltpu.roll(c, HALF, 1))
        n = jnp.where(upper == 0, n, pltpu.roll(n, HALF, 1))
        v = jnp.where(low, turn(v, c, n), v)
        kv_out[s, r, pl.ds(0, HEAD)] = v.astype(jnp.bfloat16)
        return 0

    lax.fori_loop(0, 8, own_kv, 0)
    swap = pltpu.make_async_remote_copy(
        src_ref=kv_out.at[:, :, pl.ds(0, HEAD)],
        dst_ref=kv_other,
        send_sem=kv_sem.at[0],
        recv_sem=kv_sem.at[1],
        device_id={"tp": t + 1 - 2 * upper},
        device_id_type=MESH,
    )
    swap.start()

    def queries(i, _):
        s, r = lax.div(i, 4), pl.ds(pl.multiple_of(lax.rem(i, 4) * 128, 128), 128)
        scale = scale_of(s, r)
        c, n = cosine[s, r, :], sine[s, r, :]
        for h in range(q_cols // HEAD):
            v = turn(acc[s, r, pl.ds(h * HEAD, HEAD)] * scale, c, n)
            rolled = pltpu.roll(v, HALF, 1)
            first = jnp.where(low, jnp.where(upper == 0, v, rolled), 0.0)
            second = jnp.where(low, jnp.where(upper == 0, rolled, v), 0.0)
            q_out[s, r, pl.ds(2 * h * HEAD, HEAD)] = first.astype(jnp.bfloat16)
            q_out[s, r, pl.ds((2 * h + 1) * HEAD, HEAD)] = second.astype(jnp.bfloat16)
        return 0

    lax.fori_loop(0, 8, queries, 0)
    swap.wait()
    kv_out[:, :, pl.ds(HEAD, HEAD)] = kv_other[...]
    for copy in started:
        copy.wait_send()


def project(emb, wq, wkv, gain, table, slots):
    steps, rows, width = emb.shape
    q_cols = wq.shape[1]
    heads = q_cols // HEAD
    vmem = pl.BlockSpec(memory_space=pltpu.VMEM)
    hbm = pl.BlockSpec(memory_space=pl.ANY)
    tp = RING * RING
    return pl.pallas_call(
        project_kernel,
        out_shape=(
            jax.ShapeDtypeStruct((steps, rows, heads * 2 * HEAD), jnp.bfloat16),
            jax.ShapeDtypeStruct((steps, rows, 2 * HEAD), jnp.bfloat16),
        ),
        in_specs=[hbm, hbm, hbm, vmem, vmem, vmem],
        out_specs=(vmem, vmem),
        scratch_shapes=[
            pltpu.VMEM((steps, tp, rows, width), jnp.bfloat16),
            pltpu.VMEM((tp * width, q_cols + HEAD), jnp.bfloat16),
            pltpu.VMEM((steps, rows, q_cols + HEAD), jnp.float32),
            pltpu.VMEM((steps, rows, HEAD), jnp.float32),
            pltpu.VMEM((steps, rows, HEAD), jnp.float32),
            pltpu.VMEM((steps, rows, HEAD), jnp.float32),
            pltpu.VMEM((steps, rows, HEAD), jnp.bfloat16),
            pltpu.SemaphoreType.DMA((2,)),
            pltpu.SemaphoreType.DMA((2,)),
            pltpu.SemaphoreType.DMA((2, RING + 1, 4)),
            pltpu.SemaphoreType.DMA((2, RING + 1, 4)),
            pltpu.SemaphoreType.DMA((2,)),
        ],
        compiler_params=pltpu.CompilerParams(
            collective_id=0, has_side_effects=True, vmem_limit_bytes=48 * MIB
        ),
        cost_estimate=pl.CostEstimate(
            flops=2 * steps * rows * tp * width * (q_cols + HEAD),
            bytes_accessed=300 * MIB,
            transcendentals=0,
        ),
        name="project",
    )(emb, wq, wkv, gain, table, slots)


def attend_kernel(first_b, second_b, length, begin, end, upper_ref, q, own, kv0, kv1, out):
    slot = pl.program_id(0)
    steps = q.shape[0]
    heads = q.shape[2] // (2 * HEAD)
    many = steps * heads * SUB
    n_keys = length[slot]
    lo, hi = begin[slot], end[slot]
    upper = upper_ref[0]
    factor = math.log2(math.e) / math.sqrt(HEAD)
    nt = (((1,), (1,)), ((), ()))

    def tile(i, long):
        r0 = pl.multiple_of(i * SUB, SUB)
        r = pl.ds(r0, SUB)
        query = jnp.concatenate(
            [q[s, r, pl.ds(h * 2 * HEAD, 2 * HEAD)] for s in range(steps) for h in range(heads)],
            axis=0,
        )
        mine = jnp.concatenate([own[s, r, :] for s in range(steps)], axis=0)
        pieces = [kv0[0], kv1[0]] if long else [kv0[0]]
        row = lax.broadcasted_iota(jnp.int32, (many, steps * SUB), 0)
        col = lax.broadcasted_iota(jnp.int32, (many, steps * SUB), 1)
        allowed = (lax.rem(row, SUB) == lax.rem(col, SUB)) & (
            lax.div(col, SUB) <= lax.div(row, heads * SUB)
        )
        scores = [
            jnp.where(
                allowed,
                lax.dot_general(query, mine, nt, preferred_element_type=jnp.float32),
                -jnp.inf,
            )
        ]
        for n, piece in enumerate(pieces):
            raw = lax.dot_general(query, piece, nt, preferred_element_type=jnp.float32)
            key = lax.broadcasted_iota(jnp.int32, raw.shape, 1) + n * piece.shape[0]
            scores.append(jnp.where(key < n_keys, raw, -jnp.inf))
        top = functools.reduce(
            jnp.maximum, [jnp.max(part, axis=1, keepdims=True) for part in scores]
        )
        total = jnp.zeros((many, 1), jnp.float32)
        summed = jnp.zeros((many, 2 * HEAD), jnp.float32)
        for part, piece in zip(scores, [mine] + pieces):
            weight = jnp.exp2((part - top) * factor)
            total = total + jnp.sum(weight, axis=1, keepdims=True)
            summed = summed + jnp.dot(
                weight.astype(jnp.bfloat16), piece, preferred_element_type=jnp.float32
            )
        summed = summed / total
        here, there = summed[:, :HEAD], summed[:, HEAD:]
        low = lax.broadcasted_iota(jnp.int32, here.shape, 1) < HALF
        first = jnp.where(upper == 0, here, there)
        second = jnp.where(upper == 0, there, here)
        result = jnp.where(low, pltpu.roll(first, HALF, 1), second)
        at_row = lax.broadcasted_iota(jnp.int32, (SUB, HEAD), 0) + r0
        inside = (at_row >= lo) & (at_row < hi)
        for s in range(steps):
            for h in range(heads):
                j = (s * heads + h) * SUB
                c = pl.ds(h * HEAD, HEAD)
                before = out[s, r, c].astype(jnp.float32)
                out[s, r, c] = jnp.where(inside, result[j : j + SUB], before).astype(jnp.bfloat16)
        return 0

    from_tile = lax.div(lo, SUB)
    to_tile = lax.div(hi + SUB - 1, SUB)

    @pl.when(n_keys > kv0.shape[1])
    def _():
        lax.fori_loop(from_tile, to_tile, lambda i, c: tile(i, True), 0)

    @pl.when(n_keys <= kv0.shape[1])
    def _():
        lax.fori_loop(from_tile, to_tile, lambda i, c: tile(i, False), 0)


def attend(q, own, cache, first_b, second_b, length, begin, end, upper):
    steps, rows, wide = q.shape
    whole = lambda shape: pl.BlockSpec(shape, lambda i, *_: (0,) * len(shape))
    block = (1,) + cache.shape[1:]
    return pl.pallas_call(
        attend_kernel,
        out_shape=jax.ShapeDtypeStruct((steps, rows, wide // 2), jnp.bfloat16),
        grid_spec=pltpu.PrefetchScalarGridSpec(
            num_scalar_prefetch=6,
            grid=(length.shape[0],),
            in_specs=[
                whole(q.shape),
                whole(own.shape),
                pl.BlockSpec(block, lambda i, a, b, *_: (a[i], 0, 0)),
                pl.BlockSpec(block, lambda i, a, b, *_: (b[i], 0, 0)),
            ],
            out_specs=whole((steps, rows, wide // 2)),
        ),
        compiler_params=pltpu.CompilerParams(vmem_limit_bytes=32 * MIB),
        cost_estimate=pl.CostEstimate(
            flops=8 * 10**9, bytes_accessed=60 * MIB, transcendentals=5 * 10**6
        ),
        name="attend",
    )(first_b, second_b, length, begin, end, upper, q, own, cache, cache)


def output_kernel(
    a, wo, emb, out, gathered, w, away, back,
    load_sem, w_sem, ag_send, ag_recv, rs_send, rs_recv, chunks,
):
    rows, depth = a.shape[0] // chunks, a.shape[1]
    cols = out.shape[1]
    t, x, z = place()

    def at(r):
        return pl.ds(pl.multiple_of(r * rows, rows), rows)

    def line(d):
        return {"tp": index_of(x + d, z)}

    def column(d):
        return {"tp": index_of(x, z + d)}

    def share(r, k, d):
        return pltpu.make_async_remote_copy(
            src_ref=gathered.at[0, at(r)],
            dst_ref=gathered.at[k, at(r)],
            send_sem=ag_send.at[r, k - 1],
            recv_sem=ag_recv.at[r, k - 1],
            device_id=line(d),
            device_id_type=MESH,
        )

    def forward(r, d):
        return pltpu.make_async_remote_copy(
            src_ref=gathered.at[d, at(r)],
            dst_ref=gathered.at[2, at(r)],
            send_sem=ag_send.at[r, 1],
            recv_sem=ag_recv.at[r, 1],
            device_id=line(d),
            device_id_type=MESH,
        )

    def give(r, n, d):
        return pltpu.make_async_remote_copy(
            src_ref=away.at[n, at(r)],
            dst_ref=back.at[n, at(r)],
            send_sem=rs_send.at[r, n],
            recv_sem=rs_recv.at[r, n],
            device_id=column(d),
            device_id_type=MESH,
        )

    def product(r, d):
        c = pl.ds(pl.multiple_of(lax.rem(z + d, RING) * cols, cols), cols)
        total = None
        for k in range(RING):
            part = jnp.dot(
                gathered[k, at(r), :],
                w[k, :, :, c].reshape(depth, cols),
                preferred_element_type=jnp.float32,
            )
            total = part if total is None else total + part
        return total

    def offer(r):
        share(r, 1, 1).start()
        share(r, 3, RING - 1).start()

    def arrive(r, d):
        share(r, 1, 1).wait_recv()
        share(r, 3, RING - 1).wait_recv()
        forward(r, d).start()

    greet(x, z)
    load = pltpu.make_async_copy(a, gathered.at[0], load_sem)
    load.start()
    load.wait()
    weights = [pltpu.make_async_copy(wo.at[:, k], w.at[k], w_sem.at[k]) for k in range(RING)]
    offer(0)
    offer(1)
    for copy in weights:
        copy.start()
    offer(2)
    arrive(0, 1)
    for copy in weights:
        copy.wait()

    def step(j, _):
        for parity in (0, 1):
            r = 2 * j + parity
            d = (1, RING - 1)[parity]
            e = RING - d

            @pl.when(r + 1 < chunks)
            def _():
                @pl.when(r + 3 < chunks)
                def _():
                    offer(r + 3)

                arrive(r + 1, e)

            @pl.when(r < chunks)
            def _():
                forward(r, d).wait_recv()
                away[0, at(r), :] = product(r, 2).astype(jnp.bfloat16)
                give(r, 0, d).start()
                away[2, at(r), :] = product(r, e).astype(jnp.bfloat16)
                give(r, 2, e).start()

            @pl.when((r >= 1) & (r <= chunks))
            def _():
                before = r - 1
                give(before, 0, e).wait_recv()
                total = product(before, e) + back[0, at(before), :].astype(jnp.float32)
                away[1, at(before), :] = total.astype(jnp.bfloat16)
                give(before, 1, e).start()

            @pl.when((r >= 2) & (r <= chunks + 1))
            def _():
                before = r - 2
                total = product(before, 0) + emb[at(before), :].astype(jnp.float32)
                give(before, 2, d).wait_recv()
                total = total + back[2, at(before), :].astype(jnp.float32)
                give(before, 1, d).wait_recv()
                total = total + back[1, at(before), :].astype(jnp.float32)
                out[at(before), :] = total.astype(jnp.bfloat16)

        return 0

    lax.fori_loop(0, chunks // 2 + 1, step, 0)

    def finish(r, _):
        share(r, 1, 1).wait_send()
        share(r, 3, RING - 1).wait_send()
        forward(r, 1).wait_send()
        for n in range(3):
            give(r, n, 1).wait_send()
        return 0

    lax.fori_loop(0, chunks, finish, 0)


def output(a, wo, emb, chunks):
    rows, depth = a.shape
    cols = emb.shape[1]
    vmem = pl.BlockSpec(memory_space=pltpu.VMEM)
    hbm = pl.BlockSpec(memory_space=pl.ANY)
    dma = pltpu.SemaphoreType.DMA
    return pl.pallas_call(
        functools.partial(output_kernel, chunks=chunks),
        out_shape=jax.ShapeDtypeStruct((rows, cols), jnp.bfloat16),
        in_specs=[hbm, hbm, vmem],
        out_specs=vmem,
        scratch_shapes=[
            pltpu.VMEM((RING, rows, depth), jnp.bfloat16),
            pltpu.VMEM((RING,) + wo.shape[:1] + wo.shape[2:], jnp.bfloat16),
            pltpu.VMEM((3, rows, cols), jnp.bfloat16),
            pltpu.VMEM((3, rows, cols), jnp.bfloat16),
            dma,
            dma((RING,)),
            dma((chunks, 3)),
            dma((chunks, 3)),
            dma((chunks, 3)),
            dma((chunks, 3)),
        ],
        compiler_params=pltpu.CompilerParams(
            collective_id=1, has_side_effects=True, vmem_limit_bytes=48 * MIB
        ),
        cost_estimate=pl.CostEstimate(
            flops=2 * rows * depth * RING * RING * cols, bytes_accessed=150 * MIB, transcendentals=0
        ),
        name="output",
    )(a, wo, emb)


def body(embedded, norm_gain, w_query, w_keyval, w_out, prefix_kv, prefix_len, needed, row_slot):
    group = lax.axis_index("grp")
    groups = lax.axis_size("grp")
    t, x, z = place()
    steps, rows, width = embedded.shape
    owned, longest, kv_width = prefix_kv.shape
    short = longest // 2
    n_long = owned // 2

    mine = jnp.concatenate(
        [
            prefix_kv[:n_long].reshape(2 * n_long, short, kv_width),
            prefix_kv[n_long:, :short],
        ]
    )
    theirs = lax.ppermute(mine, "tp", [(i, i ^ 1) for i in range(RING * RING)])
    per_owner = mine.shape[0]
    cache = lax.all_gather(jnp.concatenate([mine, theirs], axis=2), "grp", axis=0, tiled=True)

    piece_rows = w_out.shape[0] // groups
    quarter = w_out.shape[1] // RING
    pieces = []
    for k in range(RING):
        piece = lax.dynamic_slice(
            w_out, (group * piece_rows, lax.rem(x + k, RING) * quarter), (piece_rows, quarter)
        )
        if k:
            route = [
                (i, (i // RING + k) % RING * RING + i % RING) for i in range(RING * RING)
            ]
            piece = lax.ppermute(piece, "tp", route)
        pieces.append(piece)
    wo = lax.all_gather(jnp.stack(pieces), "grp", axis=0)

    ids = lax.dynamic_index_in_dim(needed, group, 0, keepdims=False)
    slots = ids.shape[0]
    match = ids[:, None] == jnp.arange(prefix_len.shape[0])[None, :]
    slot_len = jnp.sum(jnp.where(match, prefix_len[None, :], 0), axis=1)
    owner = ids // owned
    local = ids - owner * owned
    is_long = local < n_long
    first_b = owner * per_owner + jnp.where(is_long, 2 * local, local + n_long)
    second_b = first_b + is_long.astype(jnp.int32)
    slot_of_row = row_slot[0]
    names = jnp.arange(slots)[:, None]
    begin = jnp.sum((slot_of_row[None, :] < names).astype(jnp.int32), axis=1)
    end = jnp.sum((slot_of_row[None, :] <= names).astype(jnp.int32), axis=1)

    pair = (jnp.arange(HEAD) // 2).astype(jnp.float32)
    inverse = jnp.exp(pair * (-2.0 * math.log(ROPE_THETA) / HEAD))
    position = (slot_len[None, :] + jnp.arange(steps)[:, None]).astype(jnp.float32)
    angle = position[:, :, None] * inverse[None, None, :]
    sign = jnp.where(jnp.arange(HEAD) % 2 == 0, -1.0, 1.0)
    table = jnp.stack([jnp.cos(angle), jnp.sin(angle) * sign])

    q, own = project(
        embedded,
        w_query,
        w_keyval,
        norm_gain.reshape(RING * RING, width),
        table,
        slot_of_row[:, None],
    )
    upper = lax.rem(t, 2).astype(jnp.int32)[None]
    attended = attend(q, own, cache, first_b, second_b, slot_len, begin, end, upper)
    mixed = output(
        attended.reshape(steps * rows, width), wo, embedded.reshape(steps * rows, width), 8
    )
    return mixed.reshape(steps, rows, width)


def solution(mesh):
    in_specs = (
        P(None, "grp", "tp"),
        P(),
        P(None, "tp"),
        P(None, "tp"),
        P("tp", None),
        P("grp", None, "tp"),
        P(),
        P(),
        P("grp", None),
    )
    out_specs = P(None, "grp", "tp")
    return jax.shard_map(body, mesh=mesh, in_specs=in_specs, out_specs=out_specs, check_vma=False)
```

time: 613 us -> 248 us (0.40); the launches traced: 606 us -> 247 us
  Pallas kernels: 0 us -> 179 us
  waiting for transfers between devices: 196 us -> 30.1 us
  matrix products: 138 us -> 0 us
  local copies, waits for them, and re-layouts: 104 us -> 14 us
  other arithmetic: 76.7 us -> 3.72 us
  loops' own time: 65 us -> 0 us
    pallas_call x0 -> x3, Pallas kernels: none -> 179 us  [the longest x1 101 us: project(): pl.pallas_call(project_kernel, out_shape=(jax.ShapeDtypeStruct((steps, ro...]
    dot_general x118 -> x0, matrix products: 138 us -> none  [the longest x32 39 us: attend_slot(): jnp.einsum('rhd,ld->rhl', query_block, keys_here, preferred_element_type=...]
    reduce_scatter x2 -> x0, waiting for transfers between devices: 84.5 us -> none  [body(): lax.psum_scatter(partial_out.astype(jnp.bfloat16), 'tp', scatter_dimensio...]
    another operation x2 -> x0, loops' own time: 65 us -> none  [body(): lax.fori_loop(0, need_count, attend_slot, jnp.zeros((row_count, heads_her...]
    all_to_all x1 -> x0, waiting for transfers between devices: 48.8 us -> none  [body(): lax.all_to_all(outgoing, 'grp', split_axis=0, concat_axis=0, tiled=True)]
    dynamic_slice x96 -> x0, local copies, waits for them, and re-layouts: 38.8 us -> none  [the longest x32 19.1 us: attend_slot(): in_range = jnp.arange(length_count)[None, None, :] < slot_len[slot_index]]
    select_n x41 -> x2, other arithmetic: 21.7 us -> 0.71 us  [the longest x1 0.71 us: body(): owner = ids // owned]
    lt x32 -> x0, other arithmetic: 20.8 us -> none  [attend_slot(): in_range = jnp.arange(length_count)[None, None, :] < slot_len[slot_index]]
  transfers between devices with their start and end apart: 11 -> 6, of which waited for: 5 -> 4; matrix products, arithmetic and copies ran while one was open for 26% -> 2% of each run, Pallas kernels for 0% -> 49%
where the time goes in v1:
time: 248 us; the launch traced here: 247 us
  Pallas kernels  179 us (72%)
  waiting for transfers between devices  30.1 us (12%)
  local copies, waits for them, and re-layouts  14 us (6%)
  between operations  13.6 us (5%)
  starting transfers between devices  6.64 us (3%)
  other arithmetic  3.72 us (2%)
    pallas_call x1, Pallas kernels, project(): pl.pallas_call(project_kernel, out_shape=(jax.ShapeDtypeStruct((steps, ro...  101 us
    pallas_call x1, Pallas kernels, output(): pl.pallas_call(functools.partial(output_kernel, chunks=chunks), out_shape...  57 us
    pallas_call x1, Pallas kernels, attend(): pl.pallas_call(attend_kernel, out_shape=jax.ShapeDtypeStruct((steps, rows...  21 us
    ppermute x1, waiting for transfers between devices, body(): theirs = lax.ppermute(mine, 'tp', [(i, i ^ 1) for i in range(RING * RING)])  17.5 us
    ppermute x3, waiting for transfers between devices, body(): piece = lax.ppermute(piece, 'tp', route)  12.5 us
    unnamed x21, local copies, waits for them, and re-layouts  10.4 us
  transfers between devices with their start and end apart: 6, of which 4 were waited for; matrix products, arithmetic and copies ran while one was open for 2% of the time, Pallas kernels for 49%

profile of v1, /device:TPU:0, one launch (start us, length us, event | category | flops | bytes accessed | tf_op | source)
XLA Modules:
  0.0 246.8 jit_solution(14112180920913960978)
XLA Ops:
  6.5 1.0 slice.7
  7.5 1.1 slice.6
  8.6 0.1 pad_maximum_fusion.2
  8.7 2.1 collective-permute-start
  10.8 17.5 %collective-permute-done = bf16[12,256,128]{2,1,0:T(8,128)(2,1)S(1)} collective-permute-done((bf16[12,256,128]{2,1,0:T(8,128)(2,1)S(1)}, bf16[12,256,128]{2,1,0:T(8,128)(2,1)S(1)}, u32[]{:S(2)}, u32[]{:S(2)}) %collective-permute-start) | collective-permute-done | bytes 786464 | tf_op jit(solution)/shard_map/ppermute | solution.py:561
  28.3 1.4 pad_maximum_fusion
  29.7 0.0 all-gather.4.cloned.1.call-update
  29.7 0.0 all-gather.6.cloned.1.call-start
  29.8 1.4 dynamic-slice_bitcast_fusion
  31.3 2.8 %collective-permute-start.3 = (bf16[64,2048]{1,0:T(8,128)(2,1)S(1)}, bf16[64,2048]{1,0:T(8,128)(2,1)S(1)}, u32[]{:S(2)}, u32[]{:S(2)}) collective-permute-start(bf16[64,2048]{1,0:T(8,128)(2,1)S(1)} %get-tuple-element.17), channel_id=1, source_target_pairs={{0,12},{1,13},{2,14},{3,15},{4,0},{5,1},{6,2},{7,3},{8,4},{9,5},{1... | collective-permute-start | bytes 786440 | tf_op jit(solution)/shard_map/ppermute | solution.py:576
  34.1 0.8 collective-permute-start.2
  34.9 0.9 collective-permute-start.1
  35.8 8.9 %collective-permute-done.3 = bf16[64,2048]{1,0:T(8,128)(2,1)S(1)} collective-permute-done((bf16[64,2048]{1,0:T(8,128)(2,1)S(1)}, bf16[64,2048]{1,0:T(8,128)(2,1)S(1)}, u32[]{:S(2)}, u32[]{:S(2)}) %collective-permute-start.3) | collective-permute-done | bytes 262176 | tf_op jit(solution)/shard_map/ppermute | solution.py:576
  44.6 0.2 collective-permute-done.2
  44.9 3.5 %collective-permute-done.1 = bf16[64,2048]{1,0:T(8,128)(2,1)S(1)} collective-permute-done((bf16[64,2048]{1,0:T(8,128)(2,1)S(1)}, bf16[64,2048]{1,0:T(8,128)(2,1)S(1)}, u32[]{:S(2)}, u32[]{:S(2)}) %collective-permute-start.1) | collective-permute-done | bytes 262176 | tf_op jit(solution)/shard_map/ppermute | solution.py:576
  48.3 1.1 pad_maximum_fusion.1
  49.4 0.0 all-gather.6.cloned.1.call-update
  49.5 0.1 copy.12.slots
  49.6 0.7 and_select_fusion.2
  50.4 0.2 select_reduce_fusion.length
  50.5 0.1 multiply_cosine_fusion
  50.7 0.1 convert_reduce_fusion
  50.9 100.6 %project.1 = (bf16[2,512,1024]{2,1,0:T(8,128)(2,1)S(1)}, bf16[2,512,256]{2,1,0:T(8,128)(2,1)S(1)}) custom-call(bf16[2,512,512]{2,1,0:T(8,128)(2,1)S(1)} %copy-done.2, bf16[8192,512]{1,0:T(8,128)(2,1)} %wq.1, bf16[8192,128]{1,0:T(8,128)(2,1)S(1)} %copy-done.1, f32[16,512]{1,0:T(8,128)S(1)} %reshape.76.gain, f32[2,2,16,128]{3,2,1,0:T(8,128)S(1)} %pad_maximum_fusion.3.table, ...), custom_call_target="tpu_custom_call" | custom-call | flops 10737418240 | bytes 314572800 | tf_op jit(solution)/shard_map/project/pallas_call | solution.py:241
  151.5 1.4 copy-done.3
  152.9 0.8 copy-done.5
  153.7 4.6 %copy-done = bf16[96,256,256]{2,1,0:T(8,128)(2,1)S(1)} copy-done((bf16[96,256,256]{2,1,0:T(8,128)(2,1)S(1)}, bf16[96,256,256]{2,1,0:T(8,128)(2,1)}, u32[]{:S(2)}) %copy-start) | copy-done | bytes 12582936
  158.3 1.6 copy-done.4
  159.9 1.0 copy-done.6
  160.9 21.0 %attend.1 = bf16[2,512,512]{2,1,0:T(8,128)(2,1)S(1)} custom-call(s32[16]{0:T(128)S(1)} %get-tuple-element.12.first_b, s32[16]{0:T(128)S(1)} %get-tuple-element.11.second_b, s32[16]{0:T(128)S(1)} %select_reduce_fusion.length, s32[16]{0:T(128)S(1)} %get-tuple-element.10.begin, s32[16]{0:T(128)S(1)} %get-tuple-element.9.end, s32[1]{0:T(128)} %bitcast.2.upper_ref, ...), custom_call_target="tpu_custom_call" | custom-call | flops 8000000000 | bytes 62914560 | tf_op jit(solution)/shard_map/attend/pallas_call | solution.py:354
  182.0 0.0 all-gather.6.cloned.1.call-done
  182.0 57.0 %output.1 = bf16[1024,512]{1,0:T(8,128)(2,1)S(1)} custom-call(bf16[1024,512]{1,0:T(8,128)(2,1)S(1)} %bitcast.18, bf16[8,4,64,2048]{3,2,1,0:T(8,128)(2,1)} %bitcast.26, bf16[1024,512]{1,0:T(8,128)(2,1)S(1)} %bitcast.17), custom_call_target="tpu_custom_call" | custom-call | flops 8589934592 | bytes 157286400 | tf_op jit(solution)/shard_map/output/pallas_call | solution.py:519
  239.0 1.0 copy.14
  (22 shorter events, 0.1 us)
Async XLA Ops:
  6.5 147.2 %all-gather.4.cloned.1.call-start = ((), (), s32[]{:S(2)}) async-start(), calls=%async_computation | async-start | bytes 14155776 | tf_op jit(solution)/shard_map/all_gather | solution.py:563
  8.7 19.6 %collective-permute-start = (bf16[12,256,128]{2,1,0:T(8,128)(2,1)S(1)}, bf16[12,256,128]{2,1,0:T(8,128)(2,1)S(1)}, u32[]{:S(2)}, u32[]{:S(2)}) collective-permute-start(bf16[12,256,128]{2,1,0:T(8,128)(2,1)S(1)} %pad_maximum_fusion.2), channel_id=1, source_target_pairs={{0,1},{1,0},{2,3},{3,2},{4,5},{5,4},{6,7},{7,6},{8,9},{9,8},{10,11... | collective-permute-start | bytes 2359304 | tf_op jit(solution)/shard_map/ppermute | solution.py:561
  29.7 19.8 %copy-start.7 = (f32[8192]{0:T(1024)S(1)}, f32[8192]{0:T(1024)}, u32[]{:S(2)}) copy-start(f32[8192]{0:T(1024)} %param.10) | copy-start | bytes 98308
  29.7 19.8 %copy-start.8 = (s32[1,512]{1,0:T(1,128)S(1)}, s32[1,512]{1,0:T(1,128)}, u32[]{:S(2)}) copy-start(s32[1,512]{1,0:T(1,128)} %param.17) | copy-start | bytes 6148
  29.7 20.7 %copy-start.9 = (s32[64]{0:T(128)S(1)}, s32[64]{0:T(128)}, u32[]{:S(2)}) copy-start(s32[64]{0:T(128)} %param.15) | copy-start | bytes 772
  29.7 21.2 %copy-start.1 = (bf16[8192,128]{1,0:T(8,128)(2,1)S(1)}, bf16[8192,128]{1,0:T(8,128)(2,1)}, u32[]{:S(2)}) copy-start(bf16[8192,128]{1,0:T(8,128)(2,1)} %wkv.1) | copy-start | bytes 6291460
  29.7 21.2 %copy-start.2 = (bf16[2,512,512]{2,1,0:T(8,128)(2,1)S(1)}, bf16[2,512,512]{2,1,0:T(8,128)(2,1)}, u32[]{:S(2)}) copy-start(bf16[2,512,512]{2,1,0:T(8,128)(2,1)} %emb.1) | copy-start | bytes 3145732
  29.7 152.3 %all-gather.6.cloned.1.call-start = ((), (), s32[]{:S(2)}) async-start(), calls=%async_computation.1 | async-start | bytes 9437184 | tf_op jit(solution)/shard_map/all_gather | solution.py:578
  31.3 13.4 %collective-permute-start.3 = (bf16[64,2048]{1,0:T(8,128)(2,1)S(1)}, bf16[64,2048]{1,0:T(8,128)(2,1)S(1)}, u32[]{:S(2)}, u32[]{:S(2)}) collective-permute-start(bf16[64,2048]{1,0:T(8,128)(2,1)S(1)} %get-tuple-element.17), channel_id=1, source_target_pairs={{0,12},{1,13},{2,14},{3,15},{4,0},{5,1},{6,2},{7,3},{8,4},{9,5},{1... | collective-permute-start | bytes 786440 | tf_op jit(solution)/shard_map/ppermute | solution.py:576
  34.1 10.8 %collective-permute-start.2 = (bf16[64,2048]{1,0:T(8,128)(2,1)S(1)}, bf16[64,2048]{1,0:T(8,128)(2,1)S(1)}, u32[]{:S(2)}, u32[]{:S(2)}) collective-permute-start(bf16[64,2048]{1,0:T(8,128)(2,1)S(1)} %get-tuple-element.18), channel_id=1, source_target_pairs={{0,8},{1,9},{2,10},{3,11},{4,12},{5,13},{6,14},{7,15},{8,0},{9,1},... | collective-permute-start | bytes 786440 | tf_op jit(solution)/shard_map/ppermute | solution.py:576
  34.9 13.4 %collective-permute-start.1 = (bf16[64,2048]{1,0:T(8,128)(2,1)S(1)}, bf16[64,2048]{1,0:T(8,128)(2,1)S(1)}, u32[]{:S(2)}, u32[]{:S(2)}) collective-permute-start(bf16[64,2048]{1,0:T(8,128)(2,1)S(1)} %get-tuple-element.16), channel_id=1, source_target_pairs={{0,4},{1,5},{2,6},{3,7},{4,8},{5,9},{6,10},{7,11},{8,12},{9,13},{1... | collective-permute-start | bytes 786440 | tf_op jit(solution)/shard_map/ppermute | solution.py:576
  151.5 1.4 copy-start.3
  152.9 0.8 copy-start.5
  153.7 4.6 %copy-start = (bf16[96,256,256]{2,1,0:T(8,128)(2,1)S(1)}, bf16[96,256,256]{2,1,0:T(8,128)(2,1)}, u32[]{:S(2)}) copy-start(bf16[96,256,256]{2,1,0:T(8,128)(2,1)} %all-gather.4.cloned.1.call-done.kv0.kv1) | copy-start | bytes 37748740
  158.3 1.6 copy-start.4
  159.9 1.0 copy-start.6
Sparse Core Ops, SparseCore 0:
  29.8 69.5 all-gather.3
  101.1 50.0 all-gather.5

commit v2 on v1

v2 whole, which is shorter than its diff:
```python
import functools
import math

import jax
import jax.numpy as jnp
from jax import lax
from jax.experimental import pallas as pl
from jax.experimental.pallas import tpu as pltpu
from jax.sharding import PartitionSpec as P

HEAD = 128
HALF = 64
RING = 4
EPSILON = 1e-05
ROPE_THETA = 500000.0
SUB = 32
MIB = 1 << 20
MESH = pl.DeviceIdType.MESH
ORDER = (0, 3, 1, 2)


def place():
    t = lax.axis_index("tp")
    return t, lax.div(t, RING), lax.rem(t, RING)


def index_of(x, z):
    return lax.rem(x, RING) * RING + lax.rem(z, RING)


def greet(partners):
    barrier = pltpu.get_barrier_semaphore()
    for device in partners:
        pl.semaphore_signal(barrier, inc=1, device_id=device, device_id_type=MESH)
    pl.semaphore_wait(barrier, len(partners))


def around(x, z):
    return [{"tp": index_of(x + a, z + b)} for a, b in ((1, 0), (3, 0), (0, 1), (0, 3))]


def project_kernel(
    emb, wq, wkv, gain, row_slot, needed, lengths, prefix, prefix_halves, wo_here,
    q_out, kv_out, cache, wo, begin,
    blocks, w_q, w_kv, acc, squares, cosine, sine, kv_other, mine, table,
    load_sem, w_sem, send_sem, recv_sem, kv_sem, side_send, side_recv,
):
    rows, width = emb.shape[1], emb.shape[2]
    half = rows // 2
    q_cols = wq.shape[1]
    t, x, z = place()

    def slot_of(s, along, across):
        return index_of(x + across, z + along) if s == 0 else index_of(x + along, z + across)

    def neighbour(s, phase, d):
        on_z = (s == 0) == (phase == 0)
        return {"tp": index_of(x, z + d) if on_z else index_of(x + d, z)}

    def move(s, phase, o, kind, slot, d):
        ref = blocks.at[s, slot]
        if kind == 2:
            ref = blocks.at[s, slot, pl.ds(0, half)]
        if kind == 3:
            ref = blocks.at[s, slot, pl.ds(half, half)]
        i = o if phase else RING
        return pltpu.make_async_remote_copy(
            src_ref=ref,
            dst_ref=ref,
            send_sem=send_sem.at[s, i, kind],
            recv_sem=recv_sem.at[s, i, kind],
            device_id=neighbour(s, phase, d),
            device_id_type=MESH,
        )

    def at(s, phase, o, far):
        return slot_of(s, far, 0) if phase == 0 else slot_of(s, ORDER[o], far)

    started = []

    def start(*a):
        copy = move(*a)
        copy.start()
        started.append(copy)

    def send(s, phase, o):
        slot = at(s, phase, o, 0)
        start(s, phase, o, 0, slot, 1)
        start(s, phase, o, 1, slot, RING - 1)

    def pass_on(s, phase, o):
        back, ahead = at(s, phase, o, 3), at(s, phase, o, 1)
        move(s, phase, o, 0, back, 1).wait_recv()
        start(s, phase, o, 2, back, 1)
        move(s, phase, o, 1, ahead, 1).wait_recv()
        start(s, phase, o, 3, ahead, RING - 1)

    def opposite(s, phase, o):
        slot = at(s, phase, o, 2)
        move(s, phase, o, 2, slot, 1).wait_recv()
        move(s, phase, o, 3, slot, 1).wait_recv()

    def multiply(*todo):
        def one(i, _):
            which = lax.div(i, 2)
            s, slot = jnp.int32(todo[0][0]), todo[0][1]
            for j in range(1, len(todo)):
                s = jnp.where(which == j, todo[j][0], s)
                slot = jnp.where(which == j, todo[j][1], slot)
            r = pl.ds(pl.multiple_of(lax.rem(i, 2) * half, half), half)
            value = blocks[s, slot, r, :].astype(jnp.float32)
            square = value * value
            total = square[:, :128]
            for c in range(1, width // 128):
                total = total + square[:, c * 128 : (c + 1) * 128]
            squares[s, r, :] += total
            depth = pl.ds(pl.multiple_of(slot * width, width), width)
            scaled = (value * gain[:, depth]).astype(jnp.bfloat16)
            for ref, c in ((w_q, pl.ds(0, q_cols)), (w_kv, pl.ds(q_cols, HEAD))):
                acc[s, r, c] += jnp.dot(
                    scaled, ref[depth, :], preferred_element_type=jnp.float32
                )
            return 0

        lax.fori_loop(0, 2 * len(todo), one, 0)

    g = lax.axis_index("grp")
    y, core = lax.div(g, 2), lax.rem(g, 2)
    upper = lax.rem(t, 2)
    n_short = prefix_halves.shape[0] // 2
    n_long = 2 * n_short
    piece = wo.shape[2]
    quarter = wo.shape[3]
    cut = piece // 2
    other_half = {"tp": t + 1 - 2 * upper}
    sibling = {"grp": g + 1 - 2 * core}

    def group(a, flip=False):
        return lax.rem(y + a, RING) * 2 + (1 - core if flip else core)

    def up(d):
        return {"grp": group(d)}

    def side(n, src, dst, device):
        return pltpu.make_async_remote_copy(
            src_ref=src,
            dst_ref=dst,
            send_sem=side_send.at[n],
            recv_sem=side_recv.at[n],
            device_id=device,
            device_id_type=MESH,
        )

    def go(copy):
        copy.start()
        started.append(copy)

    def pair():
        return side(0, mine, cache.at[1, g], other_half)

    def cache_ring(h, d, group_id):
        ref = cache.at[h, group_id]
        return side(1 + 2 * h + (0 if d == 1 else 1), ref if h else mine, ref, up(d))

    def cache_forward(h, group_id):
        ref = cache.at[h, group_id]
        return side(5 + h, ref, ref, up(1 if h == 0 else RING - 1))

    def cache_sibling(h, a, flip=False):
        ref = cache.at[h, group(a, flip)]
        return side(7 + 4 * h + a, ref if h or a else mine, ref, sibling)

    def wo_line(k):
        c = pl.ds(pl.multiple_of(lax.rem(x + k, RING) * quarter, quarter), quarter)
        return side(
            14 + k, wo_here.at[g, :, c], wo.at[g, k - 1], {"tp": index_of(x + k, z)}
        )

    def wo_ring(d, group_id):
        ref = wo.at[group_id]
        return side(18 if d == 1 else 19, ref, ref, up(d))

    def wo_forward(d, group_id):
        ref = wo.at[group_id, :, pl.ds(0 if d == 1 else cut, cut)]
        return side(20 if d == 1 else 21, ref, ref, up(d))

    def wo_sibling(a, flip=False):
        ref = wo.at[group(a, flip)]
        return side(22 + a, ref, ref, sibling)

    ahead, back = 1, RING - 1

    def side_begin():
        go(pair())
        for d in (ahead, back):
            go(cache_ring(0, d, g))
        for k in (1, 2, 3):
            go(wo_line(k))

    def side_line():
        for k in (1, 2, 3):
            wo_line(k).wait_recv()
        for d in (ahead, back):
            go(wo_ring(d, g))
        go(wo_sibling(0))

    def side_pair():
        pair().wait_recv()
        for d in (ahead, back):
            go(cache_ring(1, d, g))
        for h in (0, 1):
            go(cache_sibling(h, 0))

    def side_cache(h):
        cache_ring(h, ahead, group(back)).wait_recv()
        if h == 0:
            go(cache_forward(h, group(back)))
        cache_ring(h, back, group(ahead)).wait_recv()
        if h == 1:
            go(cache_forward(h, group(ahead)))
        go(cache_sibling(h, back))
        go(cache_sibling(h, ahead))

    def side_wo():
        wo_ring(ahead, group(back)).wait_recv()
        go(wo_forward(ahead, group(back)))
        wo_ring(back, group(ahead)).wait_recv()
        go(wo_forward(back, group(ahead)))
        go(wo_sibling(back))
        go(wo_sibling(ahead))

    def side_cache_far(h):
        cache_forward(h, group(2)).wait_recv()
        go(cache_sibling(h, 2))

    def side_wo_far():
        wo_forward(ahead, group(2)).wait_recv()
        wo_forward(back, group(2)).wait_recv()
        go(wo_sibling(2))

    def side_end():
        for a in range(RING):
            for h in (0, 1):
                cache_sibling(h, a, True).wait_recv()
            wo_sibling(a, True).wait_recv()

    greet(
        around(x, z)
        + [{"tp": index_of(x + 2, z)}, sibling, up(ahead), up(back)]
    )
    loads = [pltpu.make_async_copy(emb.at[s], blocks.at[s, t], load_sem.at[s]) for s in (0, 1)]
    own_cache = [
        pltpu.make_async_copy(
            prefix.at[pl.ds(0, n_long)], mine.at[pl.ds(0, n_long)], load_sem.at[2]
        ),
        pltpu.make_async_copy(
            prefix_halves.at[pl.ds(n_short, n_short), 0],
            mine.at[pl.ds(n_long, n_short)],
            load_sem.at[3],
        ),
    ]
    for copy in loads + own_cache:
        copy.start()
    weights = [
        pltpu.make_async_copy(wq, w_q, w_sem.at[0]),
        pltpu.make_async_copy(wkv, w_kv, w_sem.at[1]),
    ]
    for copy in loads:
        copy.wait()
    for s in (0, 1):
        send(s, 0, 0)
    for copy in own_cache:
        copy.wait()
    side_begin()
    keep = pltpu.make_async_copy(mine, cache.at[0, g], load_sem.at[4])
    keep.start()
    for copy in weights:
        copy.start()
    for s in (0, 1):
        send(s, 1, 0)
    acc[...] = jnp.zeros_like(acc)
    squares[...] = jnp.zeros_like(squares)

    names = table.shape[1] // 2
    line = lax.broadcasted_iota(jnp.int32, (2 * names, HEAD), 0)
    lane = lax.broadcasted_iota(jnp.int32, (2 * names, HEAD), 1)
    position = jnp.zeros((2 * names, HEAD), jnp.int32)
    starts = []
    for n in range(names):
        length = lengths[needed[g, n]]
        position = jnp.where(line == n, length, position)
        position = jnp.where(line == names + n, length + 1, position)
        starts.append(jnp.sum(jnp.where(row_slot[...] < n, 1, 0)))
        begin[n] = starts[n]
    pair_index = lax.div(lane, 2).astype(jnp.float32)
    inverse = jnp.exp(pair_index * (-2.0 * math.log(ROPE_THETA) / HEAD))
    angle = position.astype(jnp.float32) * inverse
    table[0] = jnp.cos(angle)
    table[1] = jnp.sin(angle) * jnp.where(lax.rem(lane, 2) == 0, -1.0, 1.0)

    def spread(i, _):
        s, r0 = lax.div(i, 4), pl.multiple_of(lax.rem(i, 4) * 128, 128)
        row = lax.broadcasted_iota(jnp.int32, (128, HEAD), 0) + r0
        for k, ref in ((0, cosine), (1, sine)):
            out = jnp.zeros((128, HEAD), jnp.float32)
            for n in range(names):
                out = jnp.where(row >= starts[n], table[k, pl.ds(s * names + n, 1), :], out)
            ref[s, pl.ds(r0, 128), :] = out
        return 0

    lax.fori_loop(0, 8, spread, 0)
    for copy in weights:
        copy.wait()
    both = (0, 1)
    multiply((0, t), (1, t))
    for s in both:
        pass_on(s, 0, 0)
    for o in (1, 2):
        for s in both:
            send(s, 1, o)
    multiply(*[(s, at(s, 0, 0, d)) for d in (3, 1) for s in both])
    for s in both:
        pass_on(s, 1, 0)
    multiply(*[(s, at(s, 1, 0, d)) for d in (3, 1) for s in both])
    side_pair()
    for s in both:
        opposite(s, 0, 0)
        send(s, 1, 3)
    side_cache(0)
    multiply(*[(s, at(s, 0, 0, 2)) for s in both])
    side_line()
    for o in (1, 2, 3):
        for s in both:
            pass_on(s, 1, o)
        multiply(*[(s, at(s, 1, o, d)) for d in (3, 1) for s in both])
        if o == 1:
            side_cache(1)
        if o == 2:
            side_wo()
            side_cache_far(0)
        if o == 3:
            side_cache_far(1)
            side_wo_far()
        for s in both:
            opposite(s, 1, o - 1)
        multiply(*[(s, at(s, 1, o - 1, 2)) for s in both])
    for s in both:
        opposite(s, 1, 3)
    multiply(*[(s, at(s, 1, 3, 2)) for s in both])

    lane = lax.broadcasted_iota(jnp.int32, (128, HEAD), 1)
    low = lane < HALF
    even = lax.rem(lane, 2) == 0

    def turn(v, c, n):
        other = jnp.where(even, pltpu.roll(v, HEAD - 1, 1), pltpu.roll(v, 1, 1))
        return v * c + other * n

    def scale_of(s, r):
        mean = jnp.sum(squares[s, r, :], axis=1, keepdims=True) / (RING * RING * width)
        return lax.rsqrt(mean + EPSILON)

    def own_kv(i, _):
        s, r = lax.div(i, 4), pl.ds(pl.multiple_of(lax.rem(i, 4) * 128, 128), 128)
        v = acc[s, r, pl.ds(q_cols, HEAD)] * scale_of(s, r)
        c, n = cosine[s, r, :], sine[s, r, :]
        c = jnp.where(upper == 0, c, pltpu.roll(c, HALF, 1))
        n = jnp.where(upper == 0, n, pltpu.roll(n, HALF, 1))
        v = jnp.where(low, turn(v, c, n), v)
        kv_out[s, r, pl.ds(0, HEAD)] = v.astype(jnp.bfloat16)
        return 0

    lax.fori_loop(0, 8, own_kv, 0)
    swap = pltpu.make_async_remote_copy(
        src_ref=kv_out.at[:, :, pl.ds(0, HEAD)],
        dst_ref=kv_other,
        send_sem=kv_sem.at[0],
        recv_sem=kv_sem.at[1],
        device_id=other_half,
        device_id_type=MESH,
    )
    swap.start()

    def queries(i, _):
        s, r = lax.div(i, 4), pl.ds(pl.multiple_of(lax.rem(i, 4) * 128, 128), 128)
        scale = scale_of(s, r)
        c, n = cosine[s, r, :], sine[s, r, :]
        for h in range(q_cols // HEAD):
            v = turn(acc[s, r, pl.ds(h * HEAD, HEAD)] * scale, c, n)
            rolled = pltpu.roll(v, HALF, 1)
            first = jnp.where(low, jnp.where(upper == 0, v, rolled), 0.0)
            second = jnp.where(low, jnp.where(upper == 0, rolled, v), 0.0)
            q_out[s, r, pl.ds(2 * h * HEAD, HEAD)] = first.astype(jnp.bfloat16)
            q_out[s, r, pl.ds((2 * h + 1) * HEAD, HEAD)] = second.astype(jnp.bfloat16)
        return 0

    lax.fori_loop(0, 8, queries, 0)
    swap.wait()
    kv_out[:, :, pl.ds(HEAD, HEAD)] = kv_other[...]
    side_end()
    keep.wait()
    for copy in started:
        copy.wait_send()


def project(emb, wq, wkv, gain, row_slot, needed, lengths, prefix_kv, w_out):
    groups, names = needed.shape
    steps, rows, width = emb.shape
    q_cols = wq.shape[1]
    heads = q_cols // HEAD
    vmem = pl.BlockSpec(memory_space=pltpu.VMEM)
    hbm = pl.BlockSpec(memory_space=pl.ANY)
    smem = pl.BlockSpec(memory_space=pltpu.SMEM)
    tp = RING * RING
    owned, longest, kv_width = prefix_kv.shape
    short = longest // 2
    depth, out_cols = w_out.shape
    return pl.pallas_call(
        project_kernel,
        out_shape=(
            jax.ShapeDtypeStruct((steps, rows, heads * 2 * HEAD), jnp.bfloat16),
            jax.ShapeDtypeStruct((steps, rows, 2 * HEAD), jnp.bfloat16),
            jax.ShapeDtypeStruct((2, groups, owned * 3 // 2, short, kv_width), jnp.bfloat16),
            jax.ShapeDtypeStruct(
                (groups, RING - 1, depth // groups, out_cols // RING), jnp.bfloat16
            ),
            jax.ShapeDtypeStruct((names,), jnp.int32),
        ),
        in_specs=[hbm, hbm, hbm, vmem, vmem, smem, smem, hbm, hbm, hbm],
        out_specs=(vmem, vmem, hbm, hbm, smem),
        scratch_shapes=[
            pltpu.VMEM((steps, tp, rows, width), jnp.bfloat16),
            pltpu.VMEM((tp * width, q_cols), jnp.bfloat16),
            pltpu.VMEM((tp * width, HEAD), jnp.bfloat16),
            pltpu.VMEM((steps, rows, q_cols + HEAD), jnp.float32),
            pltpu.VMEM((steps, rows, HEAD), jnp.float32),
            pltpu.VMEM((steps, rows, HEAD), jnp.float32),
            pltpu.VMEM((steps, rows, HEAD), jnp.float32),
            pltpu.VMEM((steps, rows, HEAD), jnp.bfloat16),
            pltpu.VMEM((owned * 3 // 2, short, kv_width), jnp.bfloat16),
            pltpu.VMEM((2, 2 * names, HEAD), jnp.float32),
            pltpu.SemaphoreType.DMA((5,)),
            pltpu.SemaphoreType.DMA((2,)),
            pltpu.SemaphoreType.DMA((2, RING + 1, 4)),
            pltpu.SemaphoreType.DMA((2, RING + 1, 4)),
            pltpu.SemaphoreType.DMA((2,)),
            pltpu.SemaphoreType.DMA((26,)),
            pltpu.SemaphoreType.DMA((26,)),
        ],
        compiler_params=pltpu.CompilerParams(
            collective_id=0, has_side_effects=True, vmem_limit_bytes=58 * MIB
        ),
        cost_estimate=pl.CostEstimate(
            flops=2 * steps * rows * tp * width * (q_cols + HEAD),
            bytes_accessed=300 * MIB,
            transcendentals=0,
        ),
        name="project",
    )(
        emb, wq, wkv, gain, row_slot, needed, lengths,
        prefix_kv.reshape(2 * owned, short, kv_width),
        prefix_kv.reshape(owned, 2, short, kv_width),
        w_out.reshape(groups, depth // groups, out_cols),
    )


def attend_kernel(
    begin, needed, lengths, q, own, cache, out,
    kv, later, items, kv_sem, owned,
):
    steps, rows = q.shape[0], q.shape[1]
    heads = q.shape[2] // (2 * HEAD)
    many = steps * heads * SUB
    slots, longest = kv.shape[0], kv.shape[1]
    short = longest // 2
    n_long = owned // 2
    g = lax.axis_index("grp")
    upper = lax.rem(lax.axis_index("tp"), 2)
    factor = math.log2(math.e) / math.sqrt(HEAD)
    nt = (((1,), (1,)), ((), ()))

    def length_of(slot):
        return lengths[needed[g, slot]]

    def fetch(slot, half, size):
        prefix = needed[g, slot]
        owner, local = lax.div(prefix, owned), lax.rem(prefix, owned)
        block = owner * (owned + n_long) + jnp.where(local < n_long, 2 * local, local + n_long)
        return pltpu.make_async_copy(
            cache.at[half, pl.ds(pl.multiple_of(block * short, short), size)],
            kv.at[slot, pl.ds(0, size), pl.ds(half * HEAD, HEAD)],
            kv_sem.at[slot, half],
        )

    def each(slot, do):
        for size in (short, longest):

            @pl.when((length_of(slot) > short) == (size == longest))
            def _():
                for half in (0, 1):
                    do(fetch(slot, half, size))

        return 0

    lax.fori_loop(0, slots, lambda n, _: each(n, lambda copy: copy.start()), 0)

    def plan(slot, counts):
        lo = begin[slot]
        hi = jnp.where(slot == slots - 1, rows, begin[jnp.minimum(slot + 1, slots - 1)])
        long = length_of(slot) > short

        def add(i, counts):
            n = jnp.where(long, counts[0], counts[1])
            items[jnp.where(long, 0, 1), n] = slot * rows + i
            return counts[0] + jnp.where(long, 1, 0), counts[1] + jnp.where(long, 0, 1)

        return lax.fori_loop(lax.div(lo, SUB), lax.div(hi + SUB - 1, SUB), add, counts)

    n_items = lax.fori_loop(0, slots, plan, (jnp.int32(0), jnp.int32(0)))
    row = lax.broadcasted_iota(jnp.int32, later.shape, 0)
    col = lax.broadcasted_iota(jnp.int32, later.shape, 1)
    allowed = (lax.rem(row, SUB) == lax.rem(col, SUB)) & (
        lax.div(col, SUB) <= lax.div(row, heads * SUB)
    )
    later[...] = jnp.where(allowed, 0.0, -jnp.inf)
    lax.fori_loop(0, slots, lambda n, _: each(n, lambda copy: copy.wait()), 0)

    def run(kind, size):
        def scores_of(item):
            slot, i = lax.div(item, rows), lax.rem(item, rows)
            r = pl.ds(pl.multiple_of(i * SUB, SUB), SUB)
            query = jnp.concatenate(
                [
                    q[s, r, pl.ds(h * 2 * HEAD, 2 * HEAD)]
                    for s in range(steps)
                    for h in range(heads)
                ],
                axis=0,
            )
            mine = jnp.concatenate([own[s, r, :] for s in range(steps)], axis=0)
            parts = [
                lax.dot_general(query, mine, nt, preferred_element_type=jnp.float32) + later[...]
            ]
            for first in range(0, size, short):
                keys = kv[slot, pl.ds(first, short), :]
                raw = lax.dot_general(query, keys, nt, preferred_element_type=jnp.float32)
                if first + short == size:
                    key = lax.broadcasted_iota(jnp.int32, (1, short), 1) + first
                    raw = raw + jnp.where(key < length_of(slot), 0.0, -jnp.inf)
                parts.append(raw)
            return slot, r, i, mine, parts

        def weights_of(parts):
            top = functools.reduce(
                jnp.maximum, [jnp.max(part, axis=1, keepdims=True) for part in parts]
            )
            weights, total = [], None
            for part in parts:
                weight = jnp.exp2((part - top) * factor)
                add = jnp.sum(weight, axis=1, keepdims=True)
                total = add if total is None else total + add
                weights.append(weight.astype(jnp.bfloat16))
            return weights, total

        def values_of(slot, mine, weights, total):
            summed = jnp.dot(weights[0], mine, preferred_element_type=jnp.float32)
            for n, weight in enumerate(weights[1:]):
                values = kv[slot, pl.ds(n * short, short), :]
                summed = summed + jnp.dot(weight, values, preferred_element_type=jnp.float32)
            summed = summed / total
            here, there = summed[:, :HEAD], summed[:, HEAD:]
            low = lax.broadcasted_iota(jnp.int32, here.shape, 1) < HALF
            first = jnp.where(upper == 0, here, there)
            second = jnp.where(upper == 0, there, here)
            return jnp.where(low, pltpu.roll(first, HALF, 1), second)

        def store(slot, r, i, result):
            lo = begin[slot]
            hi = jnp.where(slot == slots - 1, rows, begin[jnp.minimum(slot + 1, slots - 1)])
            at_row = lax.broadcasted_iota(jnp.int32, (SUB, HEAD), 0) + i * SUB
            inside = (at_row >= lo) & (at_row < hi)
            for s in range(steps):
                for h in range(heads):
                    j = (s * heads + h) * SUB
                    c = pl.ds(h * HEAD, HEAD)
                    before = out[s, r, c].astype(jnp.float32)
                    out[s, r, c] = jnp.where(inside, result[j : j + SUB], before).astype(
                        jnp.bfloat16
                    )

        def two(p, _):
            last = n_items[kind] - 1
            taken = [items[kind, jnp.minimum(2 * p + e, last)] for e in (0, 1)]
            scored = [scores_of(item) for item in taken]
            soft = [weights_of(parts) for *_, parts in scored]
            results = [
                values_of(slot, mine, *pair)
                for (slot, r, i, mine, _), pair in zip(scored, soft)
            ]
            for (slot, r, i, _, _), result in zip(scored, results):
                store(slot, r, i, result)
            return 0

        lax.fori_loop(0, lax.div(n_items[kind] + 1, 2), two, 0)

    run(0, longest)
    run(1, short)


def attend(begin, needed, lengths, q, own, cache, owned):
    steps, rows, wide = q.shape
    slots = needed.shape[1]
    short, kv_width = cache.shape[3:]
    cache = cache.reshape(2, -1, kv_width)
    vmem = pl.BlockSpec(memory_space=pltpu.VMEM)
    smem = pl.BlockSpec(memory_space=pltpu.SMEM)
    heads = wide // (2 * HEAD)
    return pl.pallas_call(
        functools.partial(attend_kernel, owned=owned),
        out_shape=jax.ShapeDtypeStruct((steps, rows, wide // 2), jnp.bfloat16),
        in_specs=[smem, smem, smem, vmem, vmem, pl.BlockSpec(memory_space=pl.ANY)],
        out_specs=vmem,
        scratch_shapes=[
            pltpu.VMEM((slots, 2 * short, 2 * kv_width), jnp.bfloat16),
            pltpu.VMEM((steps * heads * SUB, steps * SUB), jnp.float32),
            pltpu.SMEM((2, rows // SUB + slots), jnp.int32),
            pltpu.SemaphoreType.DMA((slots, 2)),
        ],
        compiler_params=pltpu.CompilerParams(vmem_limit_bytes=58 * MIB),
        cost_estimate=pl.CostEstimate(
            flops=8 * 10**9, bytes_accessed=60 * MIB, transcendentals=5 * 10**6
        ),
        name="attend",
    )(begin, needed, lengths, q, own, cache)


def output_kernel(
    a, wo_here, wo, emb, out, gathered, w, away, back, middle, total,
    load_sem, w_sem, ag_send, ag_recv, rs_send, rs_recv, sizes,
):
    depth, cols = a.shape[1], out.shape[1]
    t, x, z = place()
    quarter = wo.shape[3]
    firsts = [sum(sizes[:r]) for r in range(len(sizes))]
    ahead, behind = 1, RING - 1
    ways = (ahead, behind)
    started = []

    def go(copy):
        copy.start()
        started.append(copy)

    def whole(r):
        return pl.ds(firsts[r], sizes[r])

    def part(r, u):
        return pl.ds(firsts[r] + u * (sizes[r] // 2), sizes[r] // 2)

    def line(d):
        return {"tp": index_of(x + d, z)}

    def column(d):
        return {"tp": index_of(x, z + d)}

    def remote(src, dst, sends, recvs, device):
        return pltpu.make_async_remote_copy(
            src_ref=src,
            dst_ref=dst,
            send_sem=sends,
            recv_sem=recvs,
            device_id=device,
            device_id_type=MESH,
        )

    def share(r, d):
        i = 0 if d == ahead else 1
        return remote(
            gathered.at[0, whole(r)], gathered.at[d, whole(r)],
            ag_send.at[r, i], ag_recv.at[r, i], line(d),
        )

    def forward(r, u):
        return remote(
            gathered.at[ways[u], part(r, u)], gathered.at[2, part(r, u)],
            ag_send.at[r, 2 + u], ag_recv.at[r, 2 + u], line(ways[u]),
        )

    def give(r, n, u):
        return remote(
            away.at[n, part(r, u)], back.at[n, part(r, u)],
            rs_send.at[r, 2 * n + u], rs_recv.at[r, 2 * n + u],
            column(ways[u] if n < 2 else ways[1 - u]),
        )

    def offer(r):
        for d in ways:
            go(share(r, d))

    def arrive(r):
        for u in (0, 1):
            share(r, ways[u]).wait_recv()
            go(forward(r, u))

    def product(r, d):
        c = pl.ds(pl.multiple_of(lax.rem(z + d, RING) * cols, cols), cols)
        result = None
        for k in range(RING):
            term = jnp.dot(
                gathered[k, whole(r), :],
                w[k, :, :, c].reshape(depth, cols),
                preferred_element_type=jnp.float32,
            )
            result = term if result is None else result + term
        return result

    def far(r):
        for u in (0, 1):
            forward(r, u).wait_recv()
        away[0, whole(r), :] = product(r, 2).astype(jnp.bfloat16)
        for u in (0, 1):
            go(give(r, 0, u))

    def near(r):
        n = sizes[r] // 2
        for u in (0, 1):
            value = product(r, ways[u])
            straight = value[n:] if u == 0 else value[:n]
            passing = value[:n] if u == 0 else value[n:]
            away[2, part(r, 1 - u), :] = straight.astype(jnp.bfloat16)
            go(give(r, 2, 1 - u))
            middle[part(r, u), :] = passing

    def mine(r):
        total[whole(r), :] = product(r, 0) + emb[whole(r), :].astype(jnp.float32)

    def relay(r):
        for u in (0, 1):
            give(r, 0, u).wait_recv()
            value = middle[part(r, u), :] + back[0, part(r, u), :].astype(jnp.float32)
            away[1, part(r, u), :] = value.astype(jnp.bfloat16)
            go(give(r, 1, u))

    def finish(r):
        for n in (2, 1):
            for u in (0, 1):
                give(r, n, u).wait_recv()
        value = total[whole(r), :]
        for n in (2, 1):
            value = value + back[n, whole(r), :].astype(jnp.float32)
        out[whole(r), :] = value.astype(jnp.bfloat16)

    greet(around(x, z))
    load = pltpu.make_async_copy(a, gathered.at[0], load_sem)
    load.start()
    load.wait()
    c = pl.ds(pl.multiple_of(x * quarter, quarter), quarter)
    weights = [pltpu.make_async_copy(wo_here.at[:, :, c], w.at[0], w_sem.at[0])] + [
        pltpu.make_async_copy(wo.at[:, k - 1], w.at[k], w_sem.at[k]) for k in range(1, RING)
    ]
    offer(0)
    offer(1)
    for copy in weights:
        copy.start()
    arrive(0)
    offer(2)
    for copy in weights:
        copy.wait()
    count = len(sizes)
    for r in range(count):
        if r + 1 < count:
            arrive(r + 1)
        far(r)
        if r + 3 < count:
            offer(r + 3)
        near(r)
        if r:
            relay(r - 1)
        mine(r)
        if r > 1:
            finish(r - 2)
    relay(count - 1)
    for r in (count - 2, count - 1):
        finish(r)
    for copy in started:
        copy.wait_send()


def output(a, w_out, wo, emb, sizes):
    rows, depth = a.shape
    cols = emb.shape[1]
    chunks = len(sizes)
    vmem = pl.BlockSpec(memory_space=pltpu.VMEM)
    hbm = pl.BlockSpec(memory_space=pl.ANY)
    dma = pltpu.SemaphoreType.DMA
    return pl.pallas_call(
        functools.partial(output_kernel, sizes=sizes),
        out_shape=jax.ShapeDtypeStruct((rows, cols), jnp.bfloat16),
        in_specs=[hbm, hbm, hbm, vmem],
        out_specs=vmem,
        scratch_shapes=[
            pltpu.VMEM((RING, rows, depth), jnp.bfloat16),
            pltpu.VMEM((RING,) + wo.shape[:1] + wo.shape[2:], jnp.bfloat16),
            pltpu.VMEM((3, rows, cols), jnp.bfloat16),
            pltpu.VMEM((3, rows, cols), jnp.bfloat16),
            pltpu.VMEM((rows, cols), jnp.float32),
            pltpu.VMEM((rows, cols), jnp.float32),
            dma,
            dma((RING,)),
            dma((chunks, 4)),
            dma((chunks, 4)),
            dma((chunks, 6)),
            dma((chunks, 6)),
        ],
        compiler_params=pltpu.CompilerParams(
            collective_id=1, has_side_effects=True, vmem_limit_bytes=58 * MIB
        ),
        cost_estimate=pl.CostEstimate(
            flops=2 * rows * depth * RING * RING * cols, bytes_accessed=150 * MIB, transcendentals=0
        ),
        name="output",
    )(a, w_out.reshape(wo.shape[0], wo.shape[2], w_out.shape[1]), wo, emb)


def body(embedded, norm_gain, w_query, w_keyval, w_out, prefix_kv, prefix_len, needed, row_slot):
    steps, rows, width = embedded.shape
    q, own, cache, wo, begin = project(
        embedded, w_query, w_keyval, norm_gain[None], row_slot, needed, prefix_len, prefix_kv, w_out
    )
    attended = attend(begin, needed, prefix_len, q, own, cache, prefix_kv.shape[0])
    mixed = output(
        attended.reshape(steps * rows, width),
        w_out,
        wo,
        embedded.reshape(steps * rows, width),
        (128, 256, 256, 256, 128),
    )
    return mixed.reshape(steps, rows, width)


def solution(mesh):
    in_specs = (
        P(None, "grp", "tp"),
        P(),
        P(None, "tp"),
        P(None, "tp"),
        P("tp", None),
        P("grp", None, "tp"),
        P(),
        P(),
        P("grp", None),
    )
    out_specs = P(None, "grp", "tp")
    return jax.shard_map(body, mesh=mesh, in_specs=in_specs, out_specs=out_specs, check_vma=False)
```

time: 248 us -> 203 us (0.82)
  waiting for transfers between devices: 30.1 us -> 0 us
  Pallas kernels: 179 us -> 200 us
  between operations: 13.6 us -> 0.03 us
  local copies, waits for them, and re-layouts: 14 us -> 2.26 us
  starting transfers between devices: 6.64 us -> 0 us
  other arithmetic: 3.72 us -> 0 us
    ppermute x4 -> x0, waiting for transfers between devices: 30.1 us -> none  [the longest x1 17.5 us: body(): theirs = lax.ppermute(mine, 'tp', [(i, i ^ 1) for i in range(RING * RING)])]
    pallas_call x1, Pallas kernels: 101 us -> 125 us  [project(): pl.pallas_call(project_kernel, out_shape=(jax.ShapeDtypeStruct((steps, ro...]
    unnamed x21 -> x1, local copies, waits for them, and re-layouts: 10.4 us -> 2.26 us
    ppermute x4 -> x0, starting transfers between devices: 6.59 us -> none  [the longest x3 4.51 us: body(): piece = lax.ppermute(piece, 'tp', route)]
    pallas_call x2, Pallas kernels: 78 us -> 74.9 us  [the longest x1 57.5 us: output(): pl.pallas_call(functools.partial(output_kernel, sizes=sizes), out_shape=j...]
  transfers between devices with their start and end apart: 6 -> 0, of which waited for: 4 -> 0; matrix products, arithmetic and copies ran while one was open for 2% -> 0% of each run, Pallas kernels for 49% -> 0%
where the time goes in v2:
time: 203 us; the launch traced here: 202 us
  Pallas kernels  200 us (99%)
  local copies, waits for them, and re-layouts  2.26 us (1%)
    pallas_call x1, Pallas kernels, project(): pl.pallas_call(project_kernel, out_shape=(jax.ShapeDtypeStruct((steps, ro...  125 us
    pallas_call x1, Pallas kernels, output(): pl.pallas_call(functools.partial(output_kernel, sizes=sizes), out_shape=j...  57.5 us
    pallas_call x1, Pallas kernels, attend(): pl.pallas_call(functools.partial(attend_kernel, owned=owned), out_shape=j...  17.4 us

profile of v2, /device:TPU:0, one launch (start us, length us, event | category | flops | bytes accessed | tf_op | source)
XLA Modules:
  0.0 202.3 jit_solution(13577264119747564931)
XLA Ops:
  0.0 125.1 %project.1 = (bf16[2,512,1024]{2,1,0:T(8,128)(2,1)}, bf16[2,512,256]{2,1,0:T(8,128)(2,1)}, bf16[2,8,12,256,128]{4,3,2,1,0:T(8,128)(2,1)}, bf16[8,3,64,2048]{3,2,1,0:T(8,128)(2,1)}, s32[16]{0:T(128)}) custom-call(bf16[2,512,512]{2,1,0:T(8,128)(2,1)} %emb.1, bf16[8192,512]{1,0:T(8,128)(2,1)} %wq.1, bf16[8192,128]{1,0:T(8,128)(2,1)} %wkv.1, ...), custom_call_target="tpu_custom_call" | custom-call | flops 10737418240 | bytes 314572800 | tf_op jit(solution)/shard_map/project/pallas_call | solution.py:418
  125.1 17.4 %attend.1 = bf16[2,512,512]{2,1,0:T(8,128)(2,1)} custom-call(s32[16]{0:T(128)} %get-tuple-element.10.begin, s32[8,16]{1,0:T(8,128)} %needed.3, s32[64]{0:T(128)} %lengths.3, bf16[2,512,1024]{2,1,0:T(8,128)(2,1)} %get-tuple-element.11.q, bf16[2,512,256]{2,1,0:T(8,128)(2,1)} %get-tuple-element.12.own, bf16[2,24576,128]{2,1,0:T(8,128)(2,1)} %bitcast.15), custom_call_target="tpu_custom_call" | custom-call | flops 8000000000 | bytes 62914560 | tf_op jit(solution)/shard_map/attend/pallas_call | solution.py:618
  142.5 57.5 %output.1 = bf16[1024,512]{1,0:T(8,128)(2,1)} custom-call(bf16[1024,512]{1,0:T(8,128)(2,1)} %bitcast.16, bf16[8,64,8192]{2,1,0:T(8,128)(2,1)} %bitcast.10, bf16[8,3,64,2048]{3,2,1,0:T(8,128)(2,1)} %get-tuple-element.14.wo, bf16[1024,512]{1,0:T(8,128)(2,1)} %bitcast.13), custom_call_target="tpu_custom_call" | custom-call | flops 8589934592 | bytes 157286400 | tf_op jit(solution)/shard_map/output/pallas_call | solution.py:795
  200.0 2.3 %copy.11 = bf16[2,512,512]{2,1,0:T(8,128)(2,1)} copy(bf16[2,512,512]{2,1,0:T(8,128)(2,1)} %bitcast.8) | data formatting | bytes 2097152

commit v3 on v2

--- a/solution.py
+++ b/solution.py
@@ -14,6 +14,7 @@
 EPSILON = 1e-05
 ROPE_THETA = 500000.0
 SUB = 32
+FIRST_ROWS = 544
 MIB = 1 << 20
 MESH = pl.DeviceIdType.MESH
 ORDER = (0, 3, 1, 2)
@@ -42,13 +43,16 @@
 def project_kernel(
     emb, wq, wkv, gain, row_slot, needed, lengths, prefix, prefix_halves, wo_here,
     q_out, kv_out, cache, wo, begin,
-    blocks, w_q, w_kv, acc, squares, cosine, sine, kv_other, mine, table,
+    blocks_a, blocks_b, w_q, w_kv, acc, squares, cosine, sine, kv_other, mine, table,
     load_sem, w_sem, send_sem, recv_sem, kv_sem, side_send, side_recv,
 ):
-    rows, width = emb.shape[1], emb.shape[2]
-    half = rows // 2
+    all_rows, width = emb.shape
+    rows = all_rows // 2
     q_cols = wq.shape[1]
     t, x, z = place()
+    blocks = (blocks_a, blocks_b)
+    halves = tuple(ref.shape[1] // 2 for ref in blocks)
+    firsts = (0, 2 * halves[0])
 
     def slot_of(s, along, across):
         return index_of(x + across, z + along) if s == 0 else index_of(x + along, z + across)
@@ -58,11 +62,11 @@
         return {"tp": index_of(x, z + d) if on_z else index_of(x + d, z)}
 
     def move(s, phase, o, kind, slot, d):
-        ref = blocks.at[s, slot]
+        ref = blocks[s].at[slot]
         if kind == 2:
-            ref = blocks.at[s, slot, pl.ds(0, half)]
+            ref = blocks[s].at[slot, pl.ds(0, halves[s])]
         if kind == 3:
-            ref = blocks.at[s, slot, pl.ds(half, half)]
+            ref = blocks[s].at[slot, pl.ds(halves[s], halves[s])]
         i = o if phase else RING
         return pltpu.make_async_remote_copy(
             src_ref=ref,
@@ -101,28 +105,34 @@
         move(s, phase, o, 3, slot, 1).wait_recv()
 
     def multiply(*todo):
+        for s in (0, 1):
+            slots = [slot for other, slot in todo if other == s]
+            if slots:
+                accumulate(s, slots)
+
+    def accumulate(s, slots):
+        half = halves[s]
+
         def one(i, _):
-            which = lax.div(i, 2)
-            s, slot = jnp.int32(todo[0][0]), todo[0][1]
-            for j in range(1, len(todo)):
-                s = jnp.where(which == j, todo[j][0], s)
-                slot = jnp.where(which == j, todo[j][1], slot)
-            r = pl.ds(pl.multiple_of(lax.rem(i, 2) * half, half), half)
-            value = blocks[s, slot, r, :].astype(jnp.float32)
+            which, lower = lax.div(i, 2), lax.rem(i, 2)
+            slot = slots[0]
+            for j in range(1, len(slots)):
+                slot = jnp.where(which == j, slots[j], slot)
+            value = blocks[s][slot, pl.ds(pl.multiple_of(lower * half, 16), half), :]
+            value = value.astype(jnp.float32)
+            r = pl.ds(pl.multiple_of(firsts[s] + lower * half, 16), half)
             square = value * value
             total = square[:, :128]
             for c in range(1, width // 128):
                 total = total + square[:, c * 128 : (c + 1) * 128]
-            squares[s, r, :] += total
+            squares[r, :] += total
             depth = pl.ds(pl.multiple_of(slot * width, width), width)
             scaled = (value * gain[:, depth]).astype(jnp.bfloat16)
             for ref, c in ((w_q, pl.ds(0, q_cols)), (w_kv, pl.ds(q_cols, HEAD))):
-                acc[s, r, c] += jnp.dot(
-                    scaled, ref[depth, :], preferred_element_type=jnp.float32
-                )
+                acc[r, c] += jnp.dot(scaled, ref[depth, :], preferred_element_type=jnp.float32)
             return 0
 
-        lax.fori_loop(0, 2 * len(todo), one, 0)
+        lax.fori_loop(0, 2 * len(slots), one, 0)
 
     g = lax.axis_index("grp")
     y, core = lax.div(g, 2), lax.rem(g, 2)
@@ -244,11 +254,12 @@
                 cache_sibling(h, a, True).wait_recv()
             wo_sibling(a, True).wait_recv()
 
-    greet(
-        around(x, z)
-        + [{"tp": index_of(x + 2, z)}, sibling, up(ahead), up(back)]
-    )
-    loads = [pltpu.make_async_copy(emb.at[s], blocks.at[s, t], load_sem.at[s]) for s in (0, 1)]
+    loads = [
+        pltpu.make_async_copy(
+            emb.at[pl.ds(firsts[s], 2 * halves[s])], blocks[s].at[t], load_sem.at[s]
+        )
+        for s in (0, 1)
+    ]
     own_cache = [
         pltpu.make_async_copy(
             prefix.at[pl.ds(0, n_long)], mine.at[pl.ds(0, n_long)], load_sem.at[2]
@@ -259,19 +270,23 @@
             load_sem.at[3],
         ),
     ]
-    for copy in loads + own_cache:
-        copy.start()
     weights = [
         pltpu.make_async_copy(wq, w_q, w_sem.at[0]),
         pltpu.make_async_copy(wkv, w_kv, w_sem.at[1]),
     ]
+    for copy in loads + own_cache:
+        copy.start()
+    greet(
+        around(x, z)
+        + [{"tp": index_of(x + 2, z)}, sibling, up(ahead), up(back)]
+    )
     for copy in loads:
         copy.wait()
-    for s in (0, 1):
-        send(s, 0, 0)
     for copy in own_cache:
         copy.wait()
     side_begin()
+    for s in (0, 1):
+        send(s, 0, 0)
     keep = pltpu.make_async_copy(mine, cache.at[0, g], load_sem.at[4])
     keep.start()
     for copy in weights:
@@ -299,36 +314,37 @@
     table[1] = jnp.sin(angle) * jnp.where(lax.rem(lane, 2) == 0, -1.0, 1.0)
 
     def spread(i, _):
-        s, r0 = lax.div(i, 4), pl.multiple_of(lax.rem(i, 4) * 128, 128)
-        row = lax.broadcasted_iota(jnp.int32, (128, HEAD), 0) + r0
+        s = lax.div(i * 128, rows)
+        row = lax.broadcasted_iota(jnp.int32, (128, HEAD), 0) + lax.rem(i * 128, rows)
         for k, ref in ((0, cosine), (1, sine)):
             out = jnp.zeros((128, HEAD), jnp.float32)
             for n in range(names):
                 out = jnp.where(row >= starts[n], table[k, pl.ds(s * names + n, 1), :], out)
-            ref[s, pl.ds(r0, 128), :] = out
+            ref[pl.ds(pl.multiple_of(i * 128, 128), 128), :] = out
         return 0
 
-    lax.fori_loop(0, 8, spread, 0)
+    lax.fori_loop(0, all_rows // 128, spread, 0)
     for copy in weights:
         copy.wait()
     both = (0, 1)
     multiply((0, t), (1, t))
+    side_line()
+    side_cache(0)
     for s in both:
         pass_on(s, 0, 0)
     for o in (1, 2):
         for s in both:
             send(s, 1, o)
     multiply(*[(s, at(s, 0, 0, d)) for d in (3, 1) for s in both])
+    side_pair()
     for s in both:
         pass_on(s, 1, 0)
     multiply(*[(s, at(s, 1, 0, d)) for d in (3, 1) for s in both])
-    side_pair()
     for s in both:
         opposite(s, 0, 0)
         send(s, 1, 3)
-    side_cache(0)
     multiply(*[(s, at(s, 0, 0, 2)) for s in both])
-    side_line()
+    side_wo()
     for o in (1, 2, 3):
         for s in both:
             pass_on(s, 1, o)
@@ -336,67 +352,75 @@
         if o == 1:
             side_cache(1)
         if o == 2:
-            side_wo()
             side_cache_far(0)
+            side_wo_far()
         if o == 3:
             side_cache_far(1)
-            side_wo_far()
         for s in both:
             opposite(s, 1, o - 1)
         multiply(*[(s, at(s, 1, o - 1, 2)) for s in both])
+    def turn(v, c, n):
+        even = lax.rem(lax.broadcasted_iota(jnp.int32, v.shape, 1), 2) == 0
+        other = jnp.where(even, pltpu.roll(v, HEAD - 1, 1), pltpu.roll(v, 1, 1))
+        return v * c + other * n
+
+    def scale_of(r):
+        mean = jnp.sum(squares[r, :], axis=1, keepdims=True) / (RING * RING * width)
+        return lax.rsqrt(mean + EPSILON)
+
+    def tile(s, i):
+        return pl.ds(pl.multiple_of(firsts[s] + i * halves[s], 16), halves[s])
+
+    def own_kv(s):
+        def one(i, _):
+            r = tile(s, i)
+            v = acc[r, pl.ds(q_cols, HEAD)] * scale_of(r)
+            c, n = cosine[r, :], sine[r, :]
+            low = lax.broadcasted_iota(jnp.int32, v.shape, 1) < HALF
+            c = jnp.where(upper == 0, c, pltpu.roll(c, HALF, 1))
+            n = jnp.where(upper == 0, n, pltpu.roll(n, HALF, 1))
+            kv_out[r, pl.ds(0, HEAD)] = jnp.where(low, turn(v, c, n), v).astype(jnp.bfloat16)
+            return 0
+
+        lax.fori_loop(0, 2, one, 0)
+
+    def swap(s):
+        r = pl.ds(firsts[s], 2 * halves[s])
+        return pltpu.make_async_remote_copy(
+            src_ref=kv_out.at[r, pl.ds(0, HEAD)],
+            dst_ref=kv_other.at[r],
+            send_sem=kv_sem.at[0, s],
+            recv_sem=kv_sem.at[1, s],
+            device_id=other_half,
+            device_id_type=MESH,
+        )
+
+    def queries(s):
+        def one(i, _):
+            r = tile(s, i)
+            scale = scale_of(r)
+            c, n = cosine[r, :], sine[r, :]
+            low = lax.broadcasted_iota(jnp.int32, c.shape, 1) < HALF
+            for h in range(q_cols // HEAD):
+                v = turn(acc[r, pl.ds(h * HEAD, HEAD)] * scale, c, n)
+                rolled = pltpu.roll(v, HALF, 1)
+                first = jnp.where(low, jnp.where(upper == 0, v, rolled), 0.0)
+                second = jnp.where(low, jnp.where(upper == 0, rolled, v), 0.0)
+                q_out[r, pl.ds(2 * h * HEAD, HEAD)] = first.astype(jnp.bfloat16)
+                q_out[r, pl.ds((2 * h + 1) * HEAD, HEAD)] = second.astype(jnp.bfloat16)
+            return 0
+
+        lax.fori_loop(0, 2, one, 0)
+
     for s in both:
         opposite(s, 1, 3)
-    multiply(*[(s, at(s, 1, 3, 2)) for s in both])
-
-    lane = lax.broadcasted_iota(jnp.int32, (128, HEAD), 1)
-    low = lane < HALF
-    even = lax.rem(lane, 2) == 0
-
-    def turn(v, c, n):
-        other = jnp.where(even, pltpu.roll(v, HEAD - 1, 1), pltpu.roll(v, 1, 1))
-        return v * c + other * n
-
-    def scale_of(s, r):
-        mean = jnp.sum(squares[s, r, :], axis=1, keepdims=True) / (RING * RING * width)
-        return lax.rsqrt(mean + EPSILON)
-
-    def own_kv(i, _):
-        s, r = lax.div(i, 4), pl.ds(pl.multiple_of(lax.rem(i, 4) * 128, 128), 128)
-        v = acc[s, r, pl.ds(q_cols, HEAD)] * scale_of(s, r)
-        c, n = cosine[s, r, :], sine[s, r, :]
-        c = jnp.where(upper == 0, c, pltpu.roll(c, HALF, 1))
-        n = jnp.where(upper == 0, n, pltpu.roll(n, HALF, 1))
-        v = jnp.where(low, turn(v, c, n), v)
-        kv_out[s, r, pl.ds(0, HEAD)] = v.astype(jnp.bfloat16)
-        return 0
-
-    lax.fori_loop(0, 8, own_kv, 0)
-    swap = pltpu.make_async_remote_copy(
-        src_ref=kv_out.at[:, :, pl.ds(0, HEAD)],
-        dst_ref=kv_other,
-        send_sem=kv_sem.at[0],
-        recv_sem=kv_sem.at[1],
-        device_id=other_half,
-        device_id_type=MESH,
-    )
-    swap.start()
-
-    def queries(i, _):
-        s, r = lax.div(i, 4), pl.ds(pl.multiple_of(lax.rem(i, 4) * 128, 128), 128)
-        scale = scale_of(s, r)
-        c, n = cosine[s, r, :], sine[s, r, :]
-        for h in range(q_cols // HEAD):
-            v = turn(acc[s, r, pl.ds(h * HEAD, HEAD)] * scale, c, n)
-            rolled = pltpu.roll(v, HALF, 1)
-            first = jnp.where(low, jnp.where(upper == 0, v, rolled), 0.0)
-            second = jnp.where(low, jnp.where(upper == 0, rolled, v), 0.0)
-            q_out[s, r, pl.ds(2 * h * HEAD, HEAD)] = first.astype(jnp.bfloat16)
-            q_out[s, r, pl.ds((2 * h + 1) * HEAD, HEAD)] = second.astype(jnp.bfloat16)
-        return 0
-
-    lax.fori_loop(0, 8, queries, 0)
-    swap.wait()
-    kv_out[:, :, pl.ds(HEAD, HEAD)] = kv_other[...]
+        multiply((s, at(s, 1, 3, 2)))
+        own_kv(s)
+        swap(s).start()
+        queries(s)
+    for s in both:
+        swap(s).wait()
+    kv_out[:, pl.ds(HEAD, HEAD)] = kv_other[...]
     side_end()
     keep.wait()
     for copy in started:
@@ -406,6 +430,7 @@
 def project(emb, wq, wkv, gain, row_slot, needed, lengths, prefix_kv, w_out):
     groups, names = needed.shape
     steps, rows, width = emb.shape
+    all_rows = steps * rows
     q_cols = wq.shape[1]
     heads = q_cols // HEAD
     vmem = pl.BlockSpec(memory_space=pltpu.VMEM)
@@ -418,8 +443,8 @@
     return pl.pallas_call(
         project_kernel,
         out_shape=(
-            jax.ShapeDtypeStruct((steps, rows, heads * 2 * HEAD), jnp.bfloat16),
-            jax.ShapeDtypeStruct((steps, rows, 2 * HEAD), jnp.bfloat16),
+            jax.ShapeDtypeStruct((all_rows, heads * 2 * HEAD), jnp.bfloat16),
+            jax.ShapeDtypeStruct((all_rows, 2 * HEAD), jnp.bfloat16),
             jax.ShapeDtypeStruct((2, groups, owned * 3 // 2, short, kv_width), jnp.bfloat16),
             jax.ShapeDtypeStruct(
                 (groups, RING - 1, depth // groups, out_cols // RING), jnp.bfloat16
@@ -429,21 +454,22 @@
         in_specs=[hbm, hbm, hbm, vmem, vmem, smem, smem, hbm, hbm, hbm],
         out_specs=(vmem, vmem, hbm, hbm, smem),
         scratch_shapes=[
-            pltpu.VMEM((steps, tp, rows, width), jnp.bfloat16),
+            pltpu.VMEM((tp, FIRST_ROWS, width), jnp.bfloat16),
+            pltpu.VMEM((tp, all_rows - FIRST_ROWS, width), jnp.bfloat16),
             pltpu.VMEM((tp * width, q_cols), jnp.bfloat16),
             pltpu.VMEM((tp * width, HEAD), jnp.bfloat16),
-            pltpu.VMEM((steps, rows, q_cols + HEAD), jnp.float32),
-            pltpu.VMEM((steps, rows, HEAD), jnp.float32),
-            pltpu.VMEM((steps, rows, HEAD), jnp.float32),
-            pltpu.VMEM((steps, rows, HEAD), jnp.float32),
-            pltpu.VMEM((steps, rows, HEAD), jnp.bfloat16),
+            pltpu.VMEM((all_rows, q_cols + HEAD), jnp.float32),
+            pltpu.VMEM((all_rows, HEAD), jnp.float32),
+            pltpu.VMEM((all_rows, HEAD), jnp.float32),
+            pltpu.VMEM((all_rows, HEAD), jnp.float32),
+            pltpu.VMEM((all_rows, HEAD), jnp.bfloat16),
             pltpu.VMEM((owned * 3 // 2, short, kv_width), jnp.bfloat16),
             pltpu.VMEM((2, 2 * names, HEAD), jnp.float32),
             pltpu.SemaphoreType.DMA((5,)),
             pltpu.SemaphoreType.DMA((2,)),
             pltpu.SemaphoreType.DMA((2, RING + 1, 4)),
             pltpu.SemaphoreType.DMA((2, RING + 1, 4)),
-            pltpu.SemaphoreType.DMA((2,)),
+            pltpu.SemaphoreType.DMA((2, 2)),
             pltpu.SemaphoreType.DMA((26,)),
             pltpu.SemaphoreType.DMA((26,)),
         ],
@@ -457,7 +483,7 @@
         ),
         name="project",
     )(
-        emb, wq, wkv, gain, row_slot, needed, lengths,
+        emb.reshape(all_rows, width), wq, wkv, gain, row_slot, needed, lengths,
         prefix_kv.reshape(2 * owned, short, kv_width),
         prefix_kv.reshape(owned, 2, short, kv_width),
         w_out.reshape(groups, depth // groups, out_cols),
@@ -466,7 +492,7 @@
 
 def attend_kernel(
     begin, needed, lengths, q, own, cache, out,
-    kv, later, items, kv_sem, owned,
+    kv, later, items, scores, weights, kv_sem, owned,
 ):
     steps, rows = q.shape[0], q.shape[1]
     heads = q.shape[2] // (2 * HEAD)
@@ -519,14 +545,16 @@
     n_items = lax.fori_loop(0, slots, plan, (jnp.int32(0), jnp.int32(0)))
     row = lax.broadcasted_iota(jnp.int32, later.shape, 0)
     col = lax.broadcasted_iota(jnp.int32, later.shape, 1)
-    allowed = (lax.rem(row, SUB) == lax.rem(col, SUB)) & (
-        lax.div(col, SUB) <= lax.div(row, heads * SUB)
+    allowed = (
+        (lax.rem(row, SUB) == lax.rem(col, SUB))
+        & (lax.div(col, SUB) <= lax.div(row, heads * SUB))
+        & (col < steps * SUB)
     )
     later[...] = jnp.where(allowed, 0.0, -jnp.inf)
     lax.fori_loop(0, slots, lambda n, _: each(n, lambda copy: copy.wait()), 0)
 
     def run(kind, size):
-        def scores_of(item):
+        def scores_of(e, item):
             slot, i = lax.div(item, rows), lax.rem(item, rows)
             r = pl.ds(pl.multiple_of(i * SUB, SUB), SUB)
             query = jnp.concatenate(
@@ -537,42 +565,62 @@
                 ],
                 axis=0,
             )
-            mine = jnp.concatenate([own[s, r, :] for s in range(steps)], axis=0)
-            parts = [
-                lax.dot_general(query, mine, nt, preferred_element_type=jnp.float32) + later[...]
-            ]
+            mine = jnp.concatenate(
+                [own[s, r, :] for s in range(steps)]
+                + [jnp.zeros((HEAD - steps * SUB, 2 * HEAD), jnp.bfloat16)],
+                axis=0,
+            )
+            scores[e, :, pl.ds(longest, HEAD)] = lax.dot_general(
+                query, mine, nt, preferred_element_type=jnp.float32
+            )
             for first in range(0, size, short):
                 keys = kv[slot, pl.ds(first, short), :]
-                raw = lax.dot_general(query, keys, nt, preferred_element_type=jnp.float32)
-                if first + short == size:
-                    key = lax.broadcasted_iota(jnp.int32, (1, short), 1) + first
-                    raw = raw + jnp.where(key < length_of(slot), 0.0, -jnp.inf)
-                parts.append(raw)
-            return slot, r, i, mine, parts
-
-        def weights_of(parts):
-            top = functools.reduce(
-                jnp.maximum, [jnp.max(part, axis=1, keepdims=True) for part in parts]
+                scores[e, :, pl.ds(first, short)] = lax.dot_general(
+                    query, keys, nt, preferred_element_type=jnp.float32
+                )
+            return slot, r, i, mine
+
+        def weigh(e, slot):
+            key = lax.broadcasted_iota(jnp.int32, (1, short), 1) + (size - short)
+            last = jnp.where(key < length_of(slot), 0.0, -jnp.inf)
+            totals = []
+            for m in range(0, many, SUB):
+                rows_here = pl.ds(m, SUB)
+                tiles = []
+                for first in range(0, size, HEAD):
+                    tile = scores[e, rows_here, pl.ds(first, HEAD)]
+                    if first >= size - short:
+                        c = first - (size - short)
+                        tile = tile + last[:, c : c + HEAD]
+                    tiles.append(tile)
+                tiles.append(scores[e, rows_here, pl.ds(longest, HEAD)] + later[rows_here, :])
+                top = jnp.max(functools.reduce(jnp.maximum, tiles), axis=1, keepdims=True)
+                tiles = [jnp.exp2((tile - top) * factor) for tile in tiles]
+                total = jnp.sum(functools.reduce(jnp.add, tiles), axis=1, keepdims=True)
+                totals.append(total)
+                for n, tile in enumerate(tiles):
+                    c = n * HEAD if n < size // HEAD else longest
+                    weights[e, rows_here, pl.ds(c, HEAD)] = tile.astype(jnp.bfloat16)
+            return totals
+
+        def values_of(e, slot, mine, totals):
+            summed = jnp.dot(
+                weights[e, :, pl.ds(longest, HEAD)], mine, preferred_element_type=jnp.float32
             )
-            weights, total = [], None
-            for part in parts:
-                weight = jnp.exp2((part - top) * factor)
-                add = jnp.sum(weight, axis=1, keepdims=True)
-                total = add if total is None else total + add
-                weights.append(weight.astype(jnp.bfloat16))
-            return weights, total
-
-        def values_of(slot, mine, weights, total):
-            summed = jnp.dot(weights[0], mine, preferred_element_type=jnp.float32)
-            for n, weight in enumerate(weights[1:]):
-                values = kv[slot, pl.ds(n * short, short), :]
-                summed = summed + jnp.dot(weight, values, preferred_element_type=jnp.float32)
-            summed = summed / total
-            here, there = summed[:, :HEAD], summed[:, HEAD:]
-            low = lax.broadcasted_iota(jnp.int32, here.shape, 1) < HALF
-            first = jnp.where(upper == 0, here, there)
-            second = jnp.where(upper == 0, there, here)
-            return jnp.where(low, pltpu.roll(first, HALF, 1), second)
+            summed = summed + jnp.dot(
+                weights[e, :, pl.ds(0, size)],
+                kv[slot, pl.ds(0, size), :],
+                preferred_element_type=jnp.float32,
+            )
+            out_blocks = []
+            for n, total in enumerate(totals):
+                block = summed[n * SUB : (n + 1) * SUB] / total
+                here, there = block[:, :HEAD], block[:, HEAD:]
+                low = lax.broadcasted_iota(jnp.int32, here.shape, 1) < HALF
+                first = jnp.where(upper == 0, here, there)
+                second = jnp.where(upper == 0, there, here)
+                out_blocks.append(jnp.where(low, pltpu.roll(first, HALF, 1), second))
+            return out_blocks
 
         def store(slot, r, i, result):
             lo = begin[slot]
@@ -581,23 +629,19 @@
             inside = (at_row >= lo) & (at_row < hi)
             for s in range(steps):
                 for h in range(heads):
-                    j = (s * heads + h) * SUB
                     c = pl.ds(h * HEAD, HEAD)
                     before = out[s, r, c].astype(jnp.float32)
-                    out[s, r, c] = jnp.where(inside, result[j : j + SUB], before).astype(
+                    out[s, r, c] = jnp.where(inside, result[s * heads + h], before).astype(
                         jnp.bfloat16
                     )
 
         def two(p, _):
             last = n_items[kind] - 1
             taken = [items[kind, jnp.minimum(2 * p + e, last)] for e in (0, 1)]
-            scored = [scores_of(item) for item in taken]
-            soft = [weights_of(parts) for *_, parts in scored]
-            results = [
-                values_of(slot, mine, *pair)
-                for (slot, r, i, mine, _), pair in zip(scored, soft)
-            ]
-            for (slot, r, i, _, _), result in zip(scored, results):
+            scored = [scores_of(e, taken[e]) for e in (0, 1)]
+            totals = [weigh(e, scored[e][0]) for e in (0, 1)]
+            results = [values_of(e, scored[e][0], scored[e][3], totals[e]) for e in (0, 1)]
+            for (slot, r, i, _), result in zip(scored, results):
                 store(slot, r, i, result)
             return 0
 
@@ -622,8 +666,10 @@
         out_specs=vmem,
         scratch_shapes=[
             pltpu.VMEM((slots, 2 * short, 2 * kv_width), jnp.bfloat16),
-            pltpu.VMEM((steps * heads * SUB, steps * SUB), jnp.float32),
+            pltpu.VMEM((steps * heads * SUB, HEAD), jnp.float32),
             pltpu.SMEM((2, rows // SUB + slots), jnp.int32),
+            pltpu.VMEM((2, steps * heads * SUB, 2 * short + HEAD), jnp.float32),
+            pltpu.VMEM((2, steps * heads * SUB, 2 * short + HEAD), jnp.bfloat16),
             pltpu.SemaphoreType.DMA((slots, 2)),
         ],
         compiler_params=pltpu.CompilerParams(vmem_limit_bytes=58 * MIB),
@@ -767,9 +813,9 @@
         copy.wait()
     count = len(sizes)
     for r in range(count):
+        far(r)
         if r + 1 < count:
             arrive(r + 1)
-        far(r)
         if r + 3 < count:
             offer(r + 3)
         near(r)
@@ -812,7 +858,7 @@
             dma((chunks, 6)),
         ],
         compiler_params=pltpu.CompilerParams(
-            collective_id=1, has_side_effects=True, vmem_limit_bytes=58 * MIB
+            collective_id=1, has_side_effects=True, vmem_limit_bytes=48 * MIB
         ),
         cost_estimate=pl.CostEstimate(
             flops=2 * rows * depth * RING * RING * cols, bytes_accessed=150 * MIB, transcendentals=0
@@ -826,13 +872,15 @@
     q, own, cache, wo, begin = project(
         embedded, w_query, w_keyval, norm_gain[None], row_slot, needed, prefix_len, prefix_kv, w_out
     )
+    q = q.reshape(steps, rows, q.shape[1])
+    own = own.reshape(steps, rows, own.shape[1])
     attended = attend(begin, needed, prefix_len, q, own, cache, prefix_kv.shape[0])
     mixed = output(
         attended.reshape(steps * rows, width),
         w_out,
         wo,
         embedded.reshape(steps * rows, width),
-        (128, 256, 256, 256, 128),
+        (128,) * (steps * rows // 128),
     )
     return mixed.reshape(steps, rows, width)
 

time: 203 us -> 192 us (0.946)
  Pallas kernels: 200 us -> 189 us
    pallas_call x1, Pallas kernels: 125 us -> 118 us  [project(): pl.pallas_call(project_kernel, out_shape=(jax.ShapeDtypeStruct((all_rows,...]
    pallas_call x1, Pallas kernels: 57.5 us -> 53.7 us  [output(): pl.pallas_call(functools.partial(output_kernel, sizes=sizes), out_shape=j...]
where the time goes in v3:
time: 192 us; the launch traced here: 191 us
  Pallas kernels  189 us (98%)
  local copies, waits for them, and re-layouts  2.2 us (1%)
    pallas_call x1, Pallas kernels, project(): pl.pallas_call(project_kernel, out_shape=(jax.ShapeDtypeStruct((all_rows,...  118 us
    pallas_call x1, Pallas kernels, output(): pl.pallas_call(functools.partial(output_kernel, sizes=sizes), out_shape=j...  53.7 us
    pallas_call x1, Pallas kernels, attend(): pl.pallas_call(functools.partial(attend_kernel, owned=owned), out_shape=j...  17.5 us

profile of v3, /device:TPU:0, one launch (start us, length us, event | category | flops | bytes accessed | tf_op | source)
XLA Modules:
  0.0 191.4 jit_solution(7282168196788480543)
XLA Ops:
  0.0 118.0 %project.1 = (bf16[1024,1024]{1,0:T(8,128)(2,1)}, bf16[1024,256]{1,0:T(8,128)(2,1)}, bf16[2,8,12,256,128]{4,3,2,1,0:T(8,128)(2,1)}, bf16[8,3,64,2048]{3,2,1,0:T(8,128)(2,1)}, s32[16]{0:T(128)}) custom-call(bf16[1024,512]{1,0:T(8,128)(2,1)} %bitcast.11, bf16[8192,512]{1,0:T(8,128)(2,1)} %wq.1, bf16[8192,128]{1,0:T(8,128)(2,1)} %wkv.1, f32[1,8192]{1,0:T(1,128)} %bitcast.18, ...), custom_call_target="tpu_custom_call" | custom-call | flops 10737418240 | bytes 314572800 | tf_op jit(solution)/shard_map/project/pallas_call | solution.py:443
  118.0 0.0 copy-start
  118.0 17.5 %attend.1 = bf16[2,512,512]{2,1,0:T(8,128)(2,1)} custom-call(s32[16]{0:T(128)} %get-tuple-element.10.begin, s32[8,16]{1,0:T(8,128)} %needed.3, s32[64]{0:T(128)} %lengths.3, bf16[2,512,1024]{2,1,0:T(8,128)(2,1)} %bitcast.20, bf16[2,512,256]{2,1,0:T(8,128)(2,1)} %bitcast.21, bf16[2,24576,128]{2,1,0:T(8,128)(2,1)} %bitcast.19), custom_call_target="tpu_custom_call" | custom-call | flops 8000000000 | bytes 62914560 | tf_op jit(solution)/shard_map/attend/pallas_call | solution.py:662
  135.4 0.0 copy-done
  135.5 0.0 copy-start.1
  135.5 1.2 copy-done.1
  136.7 53.7 %output.1 = bf16[1024,512]{1,0:T(8,128)(2,1)S(1)} custom-call(bf16[1024,512]{1,0:T(8,128)(2,1)S(1)} %bitcast.13, bf16[8,64,8192]{2,1,0:T(8,128)(2,1)} %bitcast.15, bf16[8,3,64,2048]{3,2,1,0:T(8,128)(2,1)} %get-tuple-element.14.wo, bf16[1024,512]{1,0:T(8,128)(2,1)S(1)} %bitcast.12), custom_call_target="tpu_custom_call" | custom-call | flops 8589934592 | bytes 157286400 | tf_op jit(solution)/shard_map/output/pallas_call | solution.py:841
  190.4 1.0 copy.11
Async XLA Ops:
  118.0 17.5 %copy-start = (bf16[2,512,512]{2,1,0:T(8,128)(2,1)S(1)}, bf16[2,512,512]{2,1,0:T(8,128)(2,1)}, u32[]{:S(2)}) copy-start(bf16[2,512,512]{2,1,0:T(8,128)(2,1)} %param.9) | copy-start | bytes 3145732
  135.5 1.2 copy-start.1

commit v4 on v3

--- a/solution.py
+++ b/solution.py
@@ -491,8 +491,8 @@
 
 
 def attend_kernel(
-    begin, needed, lengths, q, own, cache, out,
-    kv, later, items, scores, weights, kv_sem, owned,
+    begin, needed, lengths, q_here, own_here, cache, out,
+    q, own, kv, items, scores, weights, kv_sem, in_sem, owned,
 ):
     steps, rows = q.shape[0], q.shape[1]
     heads = q.shape[2] // (2 * HEAD)
@@ -528,6 +528,12 @@
 
         return 0
 
+    inputs = [
+        pltpu.make_async_copy(q_here, q, in_sem.at[0]),
+        pltpu.make_async_copy(own_here, own, in_sem.at[1]),
+    ]
+    for copy in inputs:
+        copy.start()
     lax.fori_loop(0, slots, lambda n, _: each(n, lambda copy: copy.start()), 0)
 
     def plan(slot, counts):
@@ -543,14 +549,8 @@
         return lax.fori_loop(lax.div(lo, SUB), lax.div(hi + SUB - 1, SUB), add, counts)
 
     n_items = lax.fori_loop(0, slots, plan, (jnp.int32(0), jnp.int32(0)))
-    row = lax.broadcasted_iota(jnp.int32, later.shape, 0)
-    col = lax.broadcasted_iota(jnp.int32, later.shape, 1)
-    allowed = (
-        (lax.rem(row, SUB) == lax.rem(col, SUB))
-        & (lax.div(col, SUB) <= lax.div(row, heads * SUB))
-        & (col < steps * SUB)
-    )
-    later[...] = jnp.where(allowed, 0.0, -jnp.inf)
+    for copy in inputs:
+        copy.wait()
     lax.fori_loop(0, slots, lambda n, _: each(n, lambda copy: copy.wait()), 0)
 
     def run(kind, size):
@@ -565,25 +565,25 @@
                 ],
                 axis=0,
             )
-            mine = jnp.concatenate(
-                [own[s, r, :] for s in range(steps)]
-                + [jnp.zeros((HEAD - steps * SUB, 2 * HEAD), jnp.bfloat16)],
-                axis=0,
-            )
-            scores[e, :, pl.ds(longest, HEAD)] = lax.dot_general(
-                query, mine, nt, preferred_element_type=jnp.float32
-            )
             for first in range(0, size, short):
                 keys = kv[slot, pl.ds(first, short), :]
                 scores[e, :, pl.ds(first, short)] = lax.dot_general(
                     query, keys, nt, preferred_element_type=jnp.float32
                 )
-            return slot, r, i, mine
-
-        def weigh(e, slot):
+            mine = [own[s, r, :].astype(jnp.float32) for s in range(steps)]
+            alone = []
+            for s in range(steps):
+                for h in range(heads):
+                    one = q[s, r, pl.ds(h * 2 * HEAD, 2 * HEAD)].astype(jnp.float32)
+                    alone.append(
+                        [jnp.sum(one * key, axis=1, keepdims=True) for key in mine[: s + 1]]
+                    )
+            return slot, r, i, mine, alone
+
+        def weigh(e, slot, alone):
             key = lax.broadcasted_iota(jnp.int32, (1, short), 1) + (size - short)
             last = jnp.where(key < length_of(slot), 0.0, -jnp.inf)
-            totals = []
+            totals, singles = [], []
             for m in range(0, many, SUB):
                 rows_here = pl.ds(m, SUB)
                 tiles = []
@@ -593,28 +593,30 @@
                         c = first - (size - short)
                         tile = tile + last[:, c : c + HEAD]
                     tiles.append(tile)
-                tiles.append(scores[e, rows_here, pl.ds(longest, HEAD)] + later[rows_here, :])
                 top = jnp.max(functools.reduce(jnp.maximum, tiles), axis=1, keepdims=True)
+                extra = alone[m // SUB]
+                top = functools.reduce(jnp.maximum, [top] + extra)
+                extra = [jnp.exp2((one - top) * factor) for one in extra]
                 tiles = [jnp.exp2((tile - top) * factor) for tile in tiles]
                 total = jnp.sum(functools.reduce(jnp.add, tiles), axis=1, keepdims=True)
-                totals.append(total)
+                totals.append(functools.reduce(jnp.add, [total] + extra))
+                singles.append([one.astype(jnp.bfloat16).astype(jnp.float32) for one in extra])
                 for n, tile in enumerate(tiles):
-                    c = n * HEAD if n < size // HEAD else longest
-                    weights[e, rows_here, pl.ds(c, HEAD)] = tile.astype(jnp.bfloat16)
-            return totals
-
-        def values_of(e, slot, mine, totals):
+                    weights[e, rows_here, pl.ds(n * HEAD, HEAD)] = tile.astype(jnp.bfloat16)
+            return totals, singles
+
+        def values_of(e, slot, mine, totals, singles):
             summed = jnp.dot(
-                weights[e, :, pl.ds(longest, HEAD)], mine, preferred_element_type=jnp.float32
-            )
-            summed = summed + jnp.dot(
                 weights[e, :, pl.ds(0, size)],
                 kv[slot, pl.ds(0, size), :],
                 preferred_element_type=jnp.float32,
             )
             out_blocks = []
             for n, total in enumerate(totals):
-                block = summed[n * SUB : (n + 1) * SUB] / total
+                block = summed[n * SUB : (n + 1) * SUB]
+                for one, value in zip(singles[n], mine):
+                    block = block + one * value
+                block = block / total
                 here, there = block[:, :HEAD], block[:, HEAD:]
                 low = lax.broadcasted_iota(jnp.int32, here.shape, 1) < HALF
                 first = jnp.where(upper == 0, here, there)
@@ -639,9 +641,9 @@
             last = n_items[kind] - 1
             taken = [items[kind, jnp.minimum(2 * p + e, last)] for e in (0, 1)]
             scored = [scores_of(e, taken[e]) for e in (0, 1)]
-            totals = [weigh(e, scored[e][0]) for e in (0, 1)]
-            results = [values_of(e, scored[e][0], scored[e][3], totals[e]) for e in (0, 1)]
-            for (slot, r, i, _), result in zip(scored, results):
+            soft = [weigh(e, scored[e][0], scored[e][4]) for e in (0, 1)]
+            results = [values_of(e, scored[e][0], scored[e][3], *soft[e]) for e in (0, 1)]
+            for (slot, r, i, _, _), result in zip(scored, results):
                 store(slot, r, i, result)
             return 0
 
@@ -658,21 +660,24 @@
     cache = cache.reshape(2, -1, kv_width)
     vmem = pl.BlockSpec(memory_space=pltpu.VMEM)
     smem = pl.BlockSpec(memory_space=pltpu.SMEM)
+    hbm = pl.BlockSpec(memory_space=pl.ANY)
     heads = wide // (2 * HEAD)
     return pl.pallas_call(
         functools.partial(attend_kernel, owned=owned),
         out_shape=jax.ShapeDtypeStruct((steps, rows, wide // 2), jnp.bfloat16),
-        in_specs=[smem, smem, smem, vmem, vmem, pl.BlockSpec(memory_space=pl.ANY)],
+        in_specs=[smem, smem, smem, hbm, hbm, hbm],
         out_specs=vmem,
         scratch_shapes=[
+            pltpu.VMEM(q.shape, jnp.bfloat16),
+            pltpu.VMEM(own.shape, jnp.bfloat16),
             pltpu.VMEM((slots, 2 * short, 2 * kv_width), jnp.bfloat16),
-            pltpu.VMEM((steps * heads * SUB, HEAD), jnp.float32),
             pltpu.SMEM((2, rows // SUB + slots), jnp.int32),
-            pltpu.VMEM((2, steps * heads * SUB, 2 * short + HEAD), jnp.float32),
-            pltpu.VMEM((2, steps * heads * SUB, 2 * short + HEAD), jnp.bfloat16),
+            pltpu.VMEM((2, steps * heads * SUB, 2 * short), jnp.float32),
+            pltpu.VMEM((2, steps * heads * SUB, 2 * short), jnp.bfloat16),
             pltpu.SemaphoreType.DMA((slots, 2)),
+            pltpu.SemaphoreType.DMA((2,)),
         ],
-        compiler_params=pltpu.CompilerParams(vmem_limit_bytes=58 * MIB),
+        compiler_params=pltpu.CompilerParams(vmem_limit_bytes=54 * MIB),
         cost_estimate=pl.CostEstimate(
             flops=8 * 10**9, bytes_accessed=60 * MIB, transcendentals=5 * 10**6
         ),
@@ -795,9 +800,9 @@
             value = value + back[n, whole(r), :].astype(jnp.float32)
         out[whole(r), :] = value.astype(jnp.bfloat16)
 
-    greet(around(x, z))
     load = pltpu.make_async_copy(a, gathered.at[0], load_sem)
     load.start()
+    greet(around(x, z))
     load.wait()
     c = pl.ds(pl.multiple_of(x * quarter, quarter), quarter)
     weights = [pltpu.make_async_copy(wo_here.at[:, :, c], w.at[0], w_sem.at[0])] + [

time: 192 us -> 192 us (level)
  no operation moved by 1% of the time
where the time goes in v4:
time: 192 us
  Pallas kernels  190 us (99%)
  local copies, waits for them, and re-layouts  2.2 us (1%)
    pallas_call x1, Pallas kernels, project(): pl.pallas_call(project_kernel, out_shape=(jax.ShapeDtypeStruct((all_rows,...  118 us
    pallas_call x1, Pallas kernels, output(): pl.pallas_call(functools.partial(output_kernel, sizes=sizes), out_shape=j...  55.2 us
    pallas_call x1, Pallas kernels, attend(): pl.pallas_call(functools.partial(attend_kernel, owned=owned), out_shape=j...  16.8 us

profile of v4, /device:TPU:0, one launch (start us, length us, event | category | flops | bytes accessed | tf_op | source)
XLA Modules:
  0.0 192.1 jit_solution(14407978707356120179)
XLA Ops:
  0.0 118.0 %project.1 = (bf16[1024,1024]{1,0:T(8,128)(2,1)}, bf16[1024,256]{1,0:T(8,128)(2,1)}, bf16[2,8,12,256,128]{4,3,2,1,0:T(8,128)(2,1)}, bf16[8,3,64,2048]{3,2,1,0:T(8,128)(2,1)}, s32[16]{0:T(128)}) custom-call(bf16[1024,512]{1,0:T(8,128)(2,1)} %bitcast.11, bf16[8192,512]{1,0:T(8,128)(2,1)} %wq.1, bf16[8192,128]{1,0:T(8,128)(2,1)} %wkv.1, f32[1,8192]{1,0:T(1,128)} %bitcast.18, ...), custom_call_target="tpu_custom_call" | custom-call | flops 10737418240 | bytes 314572800 | tf_op jit(solution)/shard_map/project/pallas_call | solution.py:443
  118.0 0.0 copy-start
  118.0 16.8 %attend.1 = bf16[2,512,512]{2,1,0:T(8,128)(2,1)} custom-call(s32[16]{0:T(128)} %get-tuple-element.10.begin, s32[8,16]{1,0:T(8,128)} %needed.3, s32[64]{0:T(128)} %lengths.3, bf16[2,512,1024]{2,1,0:T(8,128)(2,1)} %bitcast.20, bf16[2,512,256]{2,1,0:T(8,128)(2,1)} %bitcast.21, bf16[2,24576,128]{2,1,0:T(8,128)(2,1)} %bitcast.19), custom_call_target="tpu_custom_call" | custom-call | flops 8000000000 | bytes 62914560 | tf_op jit(solution)/shard_map/attend/pallas_call | solution.py:665
  134.8 0.0 copy-done
  134.8 0.0 copy-start.1
  134.8 1.2 copy-done.1
  136.0 55.2 %output.1 = bf16[1024,512]{1,0:T(8,128)(2,1)S(1)} custom-call(bf16[1024,512]{1,0:T(8,128)(2,1)S(1)} %bitcast.13, bf16[8,64,8192]{2,1,0:T(8,128)(2,1)} %bitcast.15, bf16[8,3,64,2048]{3,2,1,0:T(8,128)(2,1)} %get-tuple-element.14.wo, bf16[1024,512]{1,0:T(8,128)(2,1)S(1)} %bitcast.12), custom_call_target="tpu_custom_call" | custom-call | flops 8589934592 | bytes 157286400 | tf_op jit(solution)/shard_map/output/pallas_call | solution.py:846
  191.2 1.0 copy.11
Async XLA Ops:
  118.0 16.8 %copy-start = (bf16[2,512,512]{2,1,0:T(8,128)(2,1)S(1)}, bf16[2,512,512]{2,1,0:T(8,128)(2,1)}, u32[]{:S(2)}) copy-start(bf16[2,512,512]{2,1,0:T(8,128)(2,1)} %param.9) | copy-start | bytes 3145732
  134.8 1.2 copy-start.1

commit v5 on v4

--- a/solution.py
+++ b/solution.py
@@ -43,8 +43,8 @@
 def project_kernel(
     emb, wq, wkv, gain, row_slot, needed, lengths, prefix, prefix_halves, wo_here,
     q_out, kv_out, cache, wo, begin,
-    blocks_a, blocks_b, w_q, w_kv, acc, squares, cosine, sine, kv_other, mine, table,
-    load_sem, w_sem, send_sem, recv_sem, kv_sem, side_send, side_recv,
+    q_rows, blocks_a, blocks_b, w_q, w_kv, acc, squares, cosine, sine, kv_other, mine, table,
+    load_sem, w_sem, send_sem, recv_sem, kv_sem, q_sem, side_send, side_recv,
 ):
     all_rows, width = emb.shape
     rows = all_rows // 2
@@ -406,11 +406,15 @@
                 rolled = pltpu.roll(v, HALF, 1)
                 first = jnp.where(low, jnp.where(upper == 0, v, rolled), 0.0)
                 second = jnp.where(low, jnp.where(upper == 0, rolled, v), 0.0)
-                q_out[r, pl.ds(2 * h * HEAD, HEAD)] = first.astype(jnp.bfloat16)
-                q_out[r, pl.ds((2 * h + 1) * HEAD, HEAD)] = second.astype(jnp.bfloat16)
+                q_rows[r, pl.ds(2 * h * HEAD, HEAD)] = first.astype(jnp.bfloat16)
+                q_rows[r, pl.ds((2 * h + 1) * HEAD, HEAD)] = second.astype(jnp.bfloat16)
             return 0
 
         lax.fori_loop(0, 2, one, 0)
+
+    def write(s):
+        r = pl.ds(firsts[s], 2 * halves[s])
+        return pltpu.make_async_copy(q_rows.at[r], q_out.at[r], q_sem.at[s])
 
     for s in both:
         opposite(s, 1, 3)
@@ -418,11 +422,14 @@
         own_kv(s)
         swap(s).start()
         queries(s)
+        write(s).start()
     for s in both:
         swap(s).wait()
     kv_out[:, pl.ds(HEAD, HEAD)] = kv_other[...]
     side_end()
     keep.wait()
+    for s in both:
+        write(s).wait()
     for copy in started:
         copy.wait_send()
 
@@ -452,8 +459,9 @@
             jax.ShapeDtypeStruct((names,), jnp.int32),
         ),
         in_specs=[hbm, hbm, hbm, vmem, vmem, smem, smem, hbm, hbm, hbm],
-        out_specs=(vmem, vmem, hbm, hbm, smem),
+        out_specs=(hbm, vmem, hbm, hbm, smem),
         scratch_shapes=[
+            pltpu.VMEM((all_rows, heads * 2 * HEAD), jnp.bfloat16),
             pltpu.VMEM((tp, FIRST_ROWS, width), jnp.bfloat16),
             pltpu.VMEM((tp, all_rows - FIRST_ROWS, width), jnp.bfloat16),
             pltpu.VMEM((tp * width, q_cols), jnp.bfloat16),
@@ -470,6 +478,7 @@
             pltpu.SemaphoreType.DMA((2, RING + 1, 4)),
             pltpu.SemaphoreType.DMA((2, RING + 1, 4)),
             pltpu.SemaphoreType.DMA((2, 2)),
+            pltpu.SemaphoreType.DMA((2,)),
             pltpu.SemaphoreType.DMA((26,)),
             pltpu.SemaphoreType.DMA((26,)),
         ],
@@ -551,7 +560,6 @@
     n_items = lax.fori_loop(0, slots, plan, (jnp.int32(0), jnp.int32(0)))
     for copy in inputs:
         copy.wait()
-    lax.fori_loop(0, slots, lambda n, _: each(n, lambda copy: copy.wait()), 0)
 
     def run(kind, size):
         def scores_of(e, item):
@@ -649,7 +657,20 @@
 
         lax.fori_loop(0, lax.div(n_items[kind] + 1, 2), two, 0)
 
+    def arrived(size):
+        def one(slot, _):
+            @pl.when((length_of(slot) > short) == (size == longest))
+            def _():
+                for half in (0, 1):
+                    fetch(slot, half, size).wait()
+
+            return 0
+
+        lax.fori_loop(0, slots, one, 0)
+
+    arrived(longest)
     run(0, longest)
+    arrived(short)
     run(1, short)
 
 

time: 192 us -> 192 us (level)
  no operation moved by 1% of the time
where the time goes in v5:
time: 192 us; the launch traced here: 191 us
  Pallas kernels  189 us (98%)
  local copies, waits for them, and re-layouts  2.2 us (1%)
    pallas_call x1, Pallas kernels, project(): pl.pallas_call(project_kernel, out_shape=(jax.ShapeDtypeStruct((all_rows,...  117 us
    pallas_call x1, Pallas kernels, output(): pl.pallas_call(functools.partial(output_kernel, sizes=sizes), out_shape=j...  54.7 us
    pallas_call x1, Pallas kernels, attend(): pl.pallas_call(functools.partial(attend_kernel, owned=owned), out_shape=j...  16.6 us

profile of v5, /device:TPU:0, one launch (start us, length us, event | category | flops | bytes accessed | tf_op | source)
XLA Modules:
  0.0 190.9 jit_solution(10166859216926173701)
XLA Ops:
  0.0 117.3 %project.1 = (bf16[1024,1024]{1,0:T(8,128)(2,1)}, bf16[1024,256]{1,0:T(8,128)(2,1)}, bf16[2,8,12,256,128]{4,3,2,1,0:T(8,128)(2,1)}, bf16[8,3,64,2048]{3,2,1,0:T(8,128)(2,1)}, s32[16]{0:T(128)}) custom-call(bf16[1024,512]{1,0:T(8,128)(2,1)} %bitcast.11, bf16[8192,512]{1,0:T(8,128)(2,1)} %wq.1, bf16[8192,128]{1,0:T(8,128)(2,1)} %wkv.1, f32[1,8192]{1,0:T(1,128)} %bitcast.18, ...), custom_call_target="tpu_custom_call" | custom-call | flops 10737418240 | bytes 314572800 | tf_op jit(solution)/shard_map/project/pallas_call | solution.py:450
  117.3 0.0 copy-start
  117.3 16.6 %attend.1 = bf16[2,512,512]{2,1,0:T(8,128)(2,1)} custom-call(s32[16]{0:T(128)} %get-tuple-element.10.begin, s32[8,16]{1,0:T(8,128)} %needed.3, s32[64]{0:T(128)} %lengths.3, bf16[2,512,1024]{2,1,0:T(8,128)(2,1)} %bitcast.20, bf16[2,512,256]{2,1,0:T(8,128)(2,1)} %bitcast.21, bf16[2,24576,128]{2,1,0:T(8,128)(2,1)} %bitcast.19), custom_call_target="tpu_custom_call" | custom-call | flops 8000000000 | bytes 62914560 | tf_op jit(solution)/shard_map/attend/pallas_call | solution.py:686
  133.9 0.0 copy-done
  133.9 0.0 copy-start.1
  133.9 1.2 copy-done.1
  135.1 54.7 %output.1 = bf16[1024,512]{1,0:T(8,128)(2,1)S(1)} custom-call(bf16[1024,512]{1,0:T(8,128)(2,1)S(1)} %bitcast.13, bf16[8,64,8192]{2,1,0:T(8,128)(2,1)} %bitcast.15, bf16[8,3,64,2048]{3,2,1,0:T(8,128)(2,1)} %get-tuple-element.14.wo, bf16[1024,512]{1,0:T(8,128)(2,1)S(1)} %bitcast.12), custom_call_target="tpu_custom_call" | custom-call | flops 8589934592 | bytes 157286400 | tf_op jit(solution)/shard_map/output/pallas_call | solution.py:867
  189.9 1.0 copy.11
Async XLA Ops:
  117.3 16.6 %copy-start = (bf16[2,512,512]{2,1,0:T(8,128)(2,1)S(1)}, bf16[2,512,512]{2,1,0:T(8,128)(2,1)}, u32[]{:S(2)}) copy-start(bf16[2,512,512]{2,1,0:T(8,128)(2,1)} %param.9) | copy-start | bytes 3145732
  133.9 1.2 copy-start.1
